TPU v7x, 32 devices: a whole 2x2x4 slice. The times are simulated.
32 devices in a mesh: dp: 8 (over z, y), expert: 4 (over x, core).
Axes of the slice: x: 2, y: 2, z: 4, core: 2. Of those that a mesh axis runs over, the one named last changes fastest.
Arguments:
- tokens: bfloat16 [16, 1024, 384], P('dp', 'expert'), may hold values from -6 to 6
- task_ids: int32 [16], P('dp'), may hold values from 0 to 12
- attention_picks: int32 [16, 1024, 4], P('dp', 'expert'), may hold values from 0 to 14, all different within a row
- feedforward_picks: int32 [8, 4, 512, 4], P('dp', 'expert'), may hold values from 0 to 14, all different within a row; in each aligned block of 512 rows (0 to 511, 512 to 1023, ..., all dimensions but the last counted through in order) at most 256 rows name the same one
- norm_gain: float32 [2, 384], replicated, may hold values from 0.5 to 1.5
- norm_bias: float32 [2, 384], replicated, may hold values from -1.2 to 1.2
- query_weight: bfloat16 [384, 960], replicated, may hold values from -0.3125 to 0.3125
- key_weight: bfloat16 [384, 64], replicated, may hold values from -0.3125 to 0.3125
- value_weight: bfloat16 [384, 64], replicated, may hold values from -0.3125 to 0.3125
- output_weight: bfloat16 [960, 384], replicated, may hold values from -24 to 24
- attention_router: bfloat16 [13, 384, 15], replicated, may hold values from -0.15625 to 0.15625
- feedforward_router: bfloat16 [13, 384, 15], replicated, may hold values from -0.15625 to 0.15625
- expand_weight: bfloat16 [16, 384, 1536], P('expert'), may hold values from -0.3125 to 0.3125
- reduce_weight: bfloat16 [16, 1536, 384], P('expert'), may hold values from -0.3125 to 0.3125
- cotangent: bfloat16 [16, 1024, 384], P('dp', 'expert'), may hold values from -6 to 6
Outputs:
- output: bfloat16 [16, 1024, 384], P('dp', 'expert')
- grad_tokens: float32 [16, 1024, 384], P('dp', 'expert')
- grad_norm_gain: float32 [2, 384], replicated
- grad_first_bias: float32 [384], replicated
- grad_second_bias: float32 [384], replicated
- grad_query_weight: float32 [384, 960], replicated
- grad_key_weight: float32 [384, 64], replicated
- grad_value_weight: float32 [384, 64], replicated
- grad_output_weight: float32 [960, 384], replicated
- grad_attention_router: float32 [13, 384, 15], replicated
- grad_feedforward_router: float32 [13, 384, 15], replicated
- grad_expand_weight: float32 [16, 384, 1536], P('expert')
- grad_reduce_weight: float32 [16, 1536, 384], P('expert')
- usage: float32 [2, 13, 15], replicated
Inputs may be any that keep to these rules, and one draw needn't show every extreme that they name: `attention_picks`: each row names 4 different attention experts. `feedforward_picks`: each row names 4 different feed-forward experts; among the 512 rows of one device no expert is named by more than 256 rows.
All inputs are finite; a program needn't handle non-finite values.
Results may differ from a plain program's by a relative error of at most 0.014.
Values may be sent and summed in bfloat16 or wider, within the bound.
A program may use at most 192 MiB of HBM per device.

v0:
```python
import jax
import jax.numpy as jnp
from jax import lax
from jax.sharding import PartitionSpec as P

CAP = 256


EPS = 1e-06
HIGH = lax.Precision.HIGHEST


def normalize(value, gain, bias):
    mean = jnp.mean(value, -1, keepdims=True)
    centred = value - mean
    spread = jnp.mean(centred * centred, -1, keepdims=True)
    return centred * lax.rsqrt(spread + EPS) * gain + bias


def gate_weights(logits, picks_hot):
    chosen = jnp.sum(picks_hot * logits[..., None, :], -1)
    return jax.nn.softmax(chosen, -1)


def activate(value):
    return jax.nn.gelu(value, approximate=True)


def body(
    tokens,
    task_ids,
    attention_picks,
    feedforward_picks,
    norm_gain,
    norm_bias,
    query_weight,
    key_weight,
    value_weight,
    output_weight,
    attention_router,
    feedforward_router,
    expand_weight,
    reduce_weight,
    cotangent,
):
    images, patches, width = tokens.shape
    count = images * patches
    tasks = attention_router.shape[0]
    experts = attention_router.shape[2]
    head = key_weight.shape[1]
    picks = attention_picks.shape[2]
    slots = expand_weight.shape[0]
    groups = lax.axis_size("expert")
    lanes = groups * slots
    f32 = jnp.float32
    low_type = jnp.bfloat16
    inputs = tokens.astype(f32).reshape(count, width)
    expert_range = jnp.arange(experts, dtype=jnp.int32)
    task_hot = (task_ids[:, None] == jnp.arange(tasks, dtype=jnp.int32)[None, :]).astype(f32)
    task_low = task_hot.astype(low_type)
    attend_hot = (attention_picks[..., None] == expert_range).astype(f32)
    attend_low = attend_hot.astype(low_type)
    choices = feedforward_picks.reshape(count, picks)
    feed_hot = (choices[..., None] == expert_range).astype(f32)
    flat = choices.reshape(count * picks)
    marks = (flat[:, None] == expert_range[None, :]).astype(jnp.int32)
    before = jnp.cumsum(marks, axis=0) - marks
    position = flat * CAP + jnp.sum(before * marks, axis=1)
    first, first_back = jax.vjp(normalize, inputs, norm_gain[0], norm_bias[0])
    normed_one = first.astype(low_type)
    shaped_one = normed_one.reshape(images, patches, width)
    router_one = jnp.einsum(
        "it,tde->ide", task_low, attention_router, preferred_element_type=f32
    ).astype(low_type)
    logits_one = jnp.einsum("ipd,ide->ipe", shaped_one, router_one, preferred_element_type=f32)
    gates_one, gates_one_back = jax.vjp(lambda value: gate_weights(value, attend_hot), logits_one)
    queries_all = jnp.dot(normed_one, query_weight, preferred_element_type=f32).astype(low_type)
    queries_all = queries_all.reshape(images, patches, experts, head)
    queries = jnp.einsum(
        "ipke,ipeh->ipkh", attend_low, queries_all, preferred_element_type=f32
    ).astype(low_type)
    queries = queries.reshape(images, patches * picks, head)
    key_value = jnp.concatenate([key_weight, value_weight], 1)
    pair = jnp.dot(normed_one, key_value, preferred_element_type=f32).astype(low_type)
    pair = pair.reshape(images, patches, 2 * head)
    pair_all = lax.all_gather(pair, "expert", axis=1, tiled=True)
    keys_all = pair_all[:, :, :head]
    values_all = pair_all[:, :, head:]
    scores = jnp.einsum("irh,ish->irs", queries, keys_all, preferred_element_type=f32) * 0.125
    top = jnp.max(scores, -1, keepdims=True)
    expo = jnp.exp(scores - top)
    total = jnp.sum(expo, -1, keepdims=True)
    log_total = top + jnp.log(total)
    probs_low = (expo / total).astype(low_type)
    attended = jnp.einsum("irs,ish->irh", probs_low, values_all, preferred_element_type=f32)
    attended = attended.reshape(images, patches, picks, head)
    weighted = gates_one[..., None] * attended
    heads = jnp.einsum("ipke,ipkh->ipeh", attend_hot, weighted, precision=HIGH)
    heads = heads.reshape(count, experts * head).astype(low_type)
    middle = inputs + jnp.dot(heads, output_weight, preferred_element_type=f32)
    second, second_back = jax.vjp(normalize, middle, norm_gain[1], norm_bias[1])
    normed_two = second.astype(low_type)
    shaped_two = normed_two.reshape(images, patches, width)
    router_two = jnp.einsum(
        "it,tde->ide", task_low, feedforward_router, preferred_element_type=f32
    ).astype(low_type)
    logits_two = jnp.einsum(
        "ipd,ide->ipe", shaped_two, router_two, preferred_element_type=f32
    ).reshape(count, experts)
    gates_two, gates_two_back = jax.vjp(lambda value: gate_weights(value, feed_hot), logits_two)
    outgoing = (
        jnp.zeros((lanes * CAP, width), low_type)
        .at[position]
        .set(jnp.repeat(normed_two, picks, axis=0))
    )
    outgoing = outgoing.reshape(groups, slots * CAP, width)
    received = lax.all_to_all(outgoing, "expert", split_axis=0, concat_axis=0, tiled=True).reshape(
        groups, slots, CAP, width
    )
    hidden = jnp.einsum("nscd,sdf->nscf", received, expand_weight, preferred_element_type=f32)
    activated, activate_back = jax.vjp(activate, hidden)
    active_low = activated.astype(low_type)
    produced = jnp.einsum(
        "nscf,sfd->nscd", active_low, reduce_weight, preferred_element_type=f32
    ).astype(low_type)
    produced = produced.reshape(groups, slots * CAP, width)
    returned = lax.all_to_all(produced, "expert", split_axis=0, concat_axis=0, tiled=True).reshape(
        lanes * CAP, width
    )
    picked = returned[position].astype(f32).reshape(count, picks, width)
    final = middle + jnp.sum(gates_two[..., None] * picked, 1)
    output = final.astype(low_type).reshape(images, patches, width)
    grad_final = cotangent.astype(f32).reshape(count, width)
    grad_gates_two = jnp.sum(picked * grad_final[:, None, :], -1)
    grad_picked = (
        (gates_two[..., None] * grad_final[:, None, :])
        .astype(low_type)
        .reshape(count * picks, width)
    )
    grad_send = jnp.zeros((lanes * CAP, width), low_type).at[position].set(grad_picked)
    grad_send = grad_send.reshape(groups, slots * CAP, width)
    grad_produced = lax.all_to_all(
        grad_send, "expert", split_axis=0, concat_axis=0, tiled=True
    ).reshape(groups, slots, CAP, width)
    grad_reduce = jnp.einsum(
        "nscf,nscd->sfd", active_low, grad_produced, preferred_element_type=f32
    )
    grad_active = jnp.einsum(
        "nscd,sfd->nscf", grad_produced, reduce_weight, preferred_element_type=f32
    )
    grad_hidden = activate_back(grad_active)[0].astype(low_type)
    grad_expand = jnp.einsum("nscd,nscf->sdf", received, grad_hidden, preferred_element_type=f32)
    grad_rows = jnp.einsum(
        "nscf,sdf->nscd", grad_hidden, expand_weight, preferred_element_type=f32
    ).astype(low_type)
    grad_rows = grad_rows.reshape(groups, slots * CAP, width)
    grad_back = lax.all_to_all(
        grad_rows, "expert", split_axis=0, concat_axis=0, tiled=True
    ).reshape(lanes * CAP, width)
    grad_normed_two = jnp.sum(grad_back[position].astype(f32).reshape(count, picks, width), 1)
    grad_logits_two = (
        gates_two_back(grad_gates_two)[0].astype(low_type).reshape(images, patches, experts)
    )
    per_image_two = jnp.einsum(
        "ipd,ipe->ide", shaped_two, grad_logits_two, preferred_element_type=f32
    )
    grad_feed_router = jnp.einsum("it,ide->tde", task_hot, per_image_two, precision=HIGH)
    grad_normed_two = grad_normed_two + jnp.einsum(
        "ipe,ide->ipd", grad_logits_two, router_two, preferred_element_type=f32
    ).reshape(count, width)
    grad_middle_norm, grad_gain_two, grad_bias_two = second_back(grad_normed_two)
    grad_middle = grad_final + grad_middle_norm
    grad_branch = grad_middle.astype(low_type)
    grad_output = jnp.einsum("tc,td->cd", heads, grad_branch, preferred_element_type=f32)
    grad_heads = jnp.einsum(
        "td,cd->tc", grad_branch, output_weight, preferred_element_type=f32
    ).astype(low_type)
    grad_heads = grad_heads.reshape(images, patches, experts, head)
    grad_selected = jnp.einsum(
        "ipke,ipeh->ipkh", attend_low, grad_heads, preferred_element_type=f32
    )
    grad_gates_one = jnp.sum(attended * grad_selected, -1)
    grad_attended = (
        (gates_one[..., None] * grad_selected)
        .astype(low_type)
        .reshape(images, patches * picks, head)
    )
    scores_back = jnp.einsum("irh,ish->irs", queries, keys_all, preferred_element_type=f32) * 0.125
    probs_back = jnp.exp(scores_back - log_total)
    grad_values = jnp.einsum(
        "irs,irh->ish", probs_back.astype(low_type), grad_attended, preferred_element_type=f32
    )
    grad_probs = jnp.einsum("irh,ish->irs", grad_attended, values_all, preferred_element_type=f32)
    inner_sum = jnp.sum(probs_back * grad_probs, -1, keepdims=True)
    grad_scores = (probs_back * (grad_probs - inner_sum)).astype(low_type)
    grad_query_sel = (
        jnp.einsum("irs,ish->irh", grad_scores, keys_all, preferred_element_type=f32) * 0.125
    )
    grad_keys = jnp.einsum("irs,irh->ish", grad_scores, queries, preferred_element_type=f32) * 0.125
    grad_pair = jnp.concatenate([grad_keys, grad_values], -1)
    pair_sum = lax.psum_scatter(
        grad_pair.astype(jnp.bfloat16), "expert", scatter_dimension=1, tiled=True
    ).astype(jnp.float32)
    pair_sum = pair_sum.astype(low_type).reshape(count, 2 * head)
    grad_query_sel = grad_query_sel.reshape(images, patches, picks, head)
    grad_queries_all = jnp.einsum("ipke,ipkh->ipeh", attend_hot, grad_query_sel, precision=HIGH)
    grad_queries_all = grad_queries_all.astype(low_type).reshape(count, experts * head)
    grad_logits_one = gates_one_back(grad_gates_one)[0].astype(low_type)
    per_image_one = jnp.einsum(
        "ipd,ipe->ide", shaped_one, grad_logits_one, preferred_element_type=f32
    )
    grad_attend_router = jnp.einsum("it,ide->tde", task_hot, per_image_one, precision=HIGH)
    grad_query = jnp.einsum("td,tc->dc", normed_one, grad_queries_all, preferred_element_type=f32)
    grad_key_value = jnp.einsum("td,tc->dc", normed_one, pair_sum, preferred_element_type=f32)
    grad_normed_one = jnp.einsum(
        "tc,dc->td", grad_queries_all, query_weight, preferred_element_type=f32
    )
    grad_normed_one = grad_normed_one + jnp.einsum(
        "tc,dc->td", pair_sum, key_value, preferred_element_type=f32
    )
    grad_normed_one = grad_normed_one + jnp.einsum(
        "ipe,ide->ipd", grad_logits_one, router_one, preferred_element_type=f32
    ).reshape(count, width)
    grad_inputs_norm, grad_gain_one, grad_bias_one = first_back(grad_normed_one)
    grad_tokens = (grad_middle + grad_inputs_norm).reshape(images, patches, width)
    grad_gain = jnp.stack([grad_gain_one, grad_gain_two])
    grad_bias = jnp.stack([grad_bias_one, grad_bias_two])
    feed_shaped = feed_hot.reshape(images, patches, picks, experts)
    usage = jnp.stack(
        [
            jnp.einsum("it,ipke->te", task_hot, attend_hot, precision=HIGH),
            jnp.einsum("it,ipke->te", task_hot, feed_shaped, precision=HIGH),
        ]
    )
    shared = lax.psum(
        (
            grad_query,
            grad_key_value,
            grad_output,
            grad_attend_router,
            grad_feed_router,
            grad_gain,
            grad_bias,
            usage,
        ),
        ("dp", "expert"),
    )
    grad_expand_sum, grad_reduce_sum = (
        lax.psum(grad_expand.astype(jnp.bfloat16), "dp").astype(jnp.float32),
        lax.psum(grad_reduce.astype(jnp.bfloat16), "dp").astype(jnp.float32),
    )
    grad_key_sum = shared[1][:, :head]
    grad_value_sum = shared[1][:, head:]
    return (
        output,
        grad_tokens,
        shared[5],
        shared[6][0],
        shared[6][1],
        shared[0],
        grad_key_sum,
        grad_value_sum,
        shared[2],
        shared[3],
        shared[4],
        grad_expand_sum,
        grad_reduce_sum,
        shared[7],
    )


def solution(mesh):
    placed = (
        P("dp", "expert", None),
        P("dp"),
        P("dp", "expert", None),
        P("dp", "expert", None, None),
        P(),
        P(),
        P(),
        P(),
        P(),
        P(),
        P(),
        P(),
        P("expert", None, None),
        P("expert", None, None),
        P("dp", "expert", None),
    )
    return jax.shard_map(
        body,
        mesh=mesh,
        in_specs=placed,
        out_specs=(
            P("dp", "expert", None),
            P("dp", "expert", None),
            P(),
            P(),
            P(),
            P(),
            P(),
            P(),
            P(),
            P(),
            P(),
            P("expert", None, None),
            P("expert", None, None),
            P(),
        ),
        check_vma=False,
    )
```

profile of v0, /device:TPU:0, one launch (start us, length us, event | category | flops | bytes accessed | tf_op | source)
XLA Modules:
  0.0 862.4 jit_solution(16499336150467002993)
XLA Ops:
  14.2 1.8 convolution_convert_fusion.3
  16.3 3.2 copy.270
  20.1 8.6 all_gather.3
  28.8 2.6 convolution_convert_fusion.4
  35.0 2.7 fusion.27
  39.1 7.3 select_reduce_fusion.1
  47.0 5.8 convolution_convert_fusion.1
  52.9 4.1 reshape.497
  57.0 2.0 fusion.105
  60.1 4.3 reduce-window.6
  67.0 3.7 reshape.478
  70.8 12.4 %scatter_custom_fusion = bf16[4096,384]{1,0:T(8,128)(2,1)} fusion(s32[2048]{0:T(1024)S(1)} %bitcast.231, bf16[2048,384]{1,0:T(8,128)(2,1)} %reshape.478, bf16[]{:T(256)} %constant.21.clone.1), kind=kCustom, calls=%fused_computation.55 | custom fusion | bytes 3146240 | tf_op jit(solution)/shard_map/scatter | solution.py:114
  83.2 4.7 all-to-all-start
  87.9 2.1 mul.358
  90.0 5.0 mul.359
  96.0 12.9 %scatter_custom_fusion.1 = bf16[4096,384]{1,0:T(8,128)(2,1)} fusion(s32[2048]{0:T(1024)S(1)} %bitcast.232, f32[2048,384]{1,0:T(8,128)} %mul.359, f32[2048]{0:T(1024)S(1)} %div.113, bf16[]{:T(256)} %constant.21.clone.1), kind=kCustom, calls=%fused_computation.52 | custom fusion | flops 1572864 | bytes 6299650 | tf_op jit(solution)/shard_map/scatter | solution.py:140
  108.9 15.9 %all-to-all-done = bf16[4,1024,384]{2,1,0:T(8,128)(2,1)} async-done(((bf16[4,1024,384]{2,1,0:T(8,128)(2,1)}), bf16[4,1024,384]{2,1,0:T(8,128)(2,1)}, u32[]{:S(2)}, u32[]{:S(2)}) %all-to-all-start) | async-done | bytes 3145760 | tf_op jit(solution)/shard_map/all_to_all | solution.py:117
  124.8 4.8 all-to-all-start.2
  129.7 19.9 %fusion.11 = (bf16[4,4,256,1536]{3,2,0,1:T(8,128)(2,1)}, f32[4,4,256,1536]{3,2,1,0:T(8,128)}) fusion(bf16[4,384,1536]{2,1,0:T(8,128)(2,1)} %param.27, bf16[4,4,256,384]{3,2,1,0:T(8,128)(2,1)} %bitcast.11), kind=kOutput, calls=%fused_computation.20 | convolution fusion | flops 4888461312 | bytes 45613056 | tf_op jit(solution)/shard_map/nscd,sdf->nscf/dot_general | solution.py:120
  149.6 17.0 %all-to-all-done.2 = bf16[4,1024,384]{2,1,0:T(8,128)(2,1)} async-done(((bf16[4,1024,384]{2,1,0:T(8,128)(2,1)}), bf16[4,1024,384]{2,1,0:T(8,128)(2,1)}, u32[]{:S(2)}, u32[]{:S(2)}) %all-to-all-start.2) | async-done | bytes 3145760 | tf_op jit(solution)/shard_map/all_to_all | solution.py:142
  166.7 27.0 %fusion.7 = bf16[4,4,256,1536]{3,2,0,1:T(8,128)(2,1)} fusion(f32[4,4,256,1536]{3,2,1,0:T(8,128)} %get-tuple-element.142, bf16[4,1536,384]{2,1,0:T(8,128)(2,1)} %param.28, bf16[4,4,256,384]{3,2,1,0:T(8,128)(2,1)} %bitcast.24), kind=kOutput, calls=%fused_computation.13 | convolution fusion | flops 4957667328 | bytes 45613056 | tf_op jit(solution)/shard_map/nscd,sfd->nscf/dot_general | solution.py:148
  193.6 11.0 %convert_bitcast_fusion = bf16[4,4,256,384]{3,2,0,1:T(8,128)(2,1)S(1)} fusion(bf16[4,4,256,1536]{3,2,0,1:T(8,128)(2,1)} %fusion.7, bf16[4,384,1536]{2,1,0:T(8,128)(2,1)} %param.27), kind=kOutput, calls=%fused_computation.44 | convolution fusion | flops 4833411072 | bytes 20447232 | tf_op jit(solution)/shard_map/nscf,sdf->nscd/dot_general | solution.py:153
  204.7 2.0 copy.287
  206.6 4.7 all-to-all-start.3
  211.3 11.0 %convert_bitcast_fusion.1 = bf16[4,4,256,384]{3,2,0,1:T(8,128)(2,1)S(1)} fusion(bf16[4,4,256,1536]{3,2,0,1:T(8,128)(2,1)} %get-tuple-element.141, bf16[4,1536,384]{2,1,0:T(8,128)(2,1)} %param.28), kind=kOutput, calls=%fused_computation.47 | convolution fusion | flops 4833411072 | bytes 20447232 | tf_op jit(solution)/shard_map/nscf,sfd->nscd/dot_general | solution.py:123
  222.3 2.0 copy.284
  224.4 23.9 %all-to-all-done.3 = bf16[4,1024,384]{2,1,0:T(8,128)(2,1)} async-done(((bf16[4,1024,384]{2,1,0:T(8,128)(2,1)}), bf16[4,1024,384]{2,1,0:T(8,128)(2,1)}, u32[]{:S(2)}, u32[]{:S(2)}) %all-to-all-start.3) | async-done | bytes 3145760 | tf_op jit(solution)/shard_map/all_to_all | solution.py:157
  248.3 4.6 all-to-all-start.1
  255.1 11.6 %gather_fusion.1 = bf16[2048,384]{1,0:T(8,128)(2,1)} fusion(bf16[4096,384]{1,0:T(8,128)(2,1)} %bitcast.30, s32[2048]{0:T(1024)S(1)} %broadcast_clamp_fusion), kind=kCustom, calls=%fused_computation.1 | custom fusion | bytes 3153920 | tf_op jit(solution)/shard_map/gather | solution.py:160
  266.7 4.2 reshape.457
  270.9 3.8 reduce_sum.281
  274.7 15.3 %all-to-all-done.1 = bf16[4,1024,384]{2,1,0:T(8,128)(2,1)} async-done(((bf16[4,1024,384]{2,1,0:T(8,128)(2,1)}), bf16[4,1024,384]{2,1,0:T(8,128)(2,1)}, u32[]{:S(2)}, u32[]{:S(2)}) %all-to-all-start.1) | async-done | bytes 3145760 | tf_op jit(solution)/shard_map/all_to_all | solution.py:127
  289.9 11.1 %gather_fusion = bf16[2048,384]{1,0:T(8,128)(2,1)} fusion(bf16[4096,384]{1,0:T(8,128)(2,1)} %bitcast.19, s32[2048]{0:T(1024)S(1)} %broadcast_clamp_fusion), kind=kCustom, calls=%fused_computation | custom fusion | bytes 3153920 | tf_op jit(solution)/shard_map/gather | solution.py:130
  301.1 4.3 reshape.454
  305.3 6.5 multiply_reduce_fusion.2
  316.0 1.7 multiply_reduce_fusion.5
  318.3 2.3 fusion.102
  322.4 1.6 convolution_convert_fusion.2
  324.1 2.5 reshape.443
  326.6 3.2 copy.292
  329.8 3.5 multiply_convert_fusion.3
  333.4 4.8 multiply_reduce_fusion
  338.2 2.3 fusion.42
  340.6 2.5 multiply_convert_fusion
  344.1 2.1 fusion.45
  346.9 3.5 convert_reduce_fusion
  352.4 6.5 convolution_convert_fusion
  358.8 4.1 reshape.498
  362.9 1.8 pad_maximum_fusion
  368.1 1.8 fusion.107
  369.9 3.1 fusion.108
  373.0 13.9 %reduce-scatter.2.cloned.1.call-done = bf16[2,256,128]{1,2,0:T(8,128)(2,1)} async-done(((bf16[2,1024,128]{1,2,0:T(8,128)(2,1)}), bf16[2,256,128]{1,2,0:T(8,128)(2,1)}) %reduce-scatter.2.cloned.1.call-update) | async-done | bytes 131088 | tf_op jit(solution)/shard_map/reduce_scatter | solution.py:201
  386.9 1.9 convolution_bitcast_fusion
  388.9 10.7 %bitcast_convert_fusion.1 = bf16[4,384,1536]{2,1,0:T(8,128)(2,1)} fusion(bf16[4,4,256,384]{3,2,1,0:T(8,128)(2,1)} %bitcast.11, bf16[4,4,256,1536]{3,2,0,1:T(8,128)(2,1)} %fusion.7), kind=kOutput, calls=%fused_computation.24 | convolution fusion | flops 4834197504 | bytes 20447232 | tf_op jit(solution)/shard_map/nscd,nscf->sdf/dot_general | solution.py:152
  399.6 12.6 %bitcast_convert_fusion = bf16[4,1536,384]{2,1,0:T(8,128)(2,1)} fusion(bf16[4,4,256,1536]{3,2,0,1:T(8,128)(2,1)} %get-tuple-element.141, bf16[4,4,256,384]{3,2,1,0:T(8,128)(2,1)} %bitcast.24), kind=kOutput, calls=%fused_computation.23 | convolution fusion | flops 4834197504 | bytes 20447232 | tf_op jit(solution)/shard_map/nscf,nscd->sfd/dot_general | solution.py:145
  414.6 2.8 fusion.106
  417.6 1.8 fusion.101
  420.0 40.0 %all-reduce = (f32[2,384]{1,0:T(2,128)}, f32[2,384]{1,0:T(2,128)S(1)}, f32[2,13,15]{2,1,0:T(8,128)S(1)}) all-reduce(f32[2,384]{1,0:T(2,128)S(1)} %pad_maximum_fusion.2, f32[2,384]{1,0:T(2,128)S(1)} %pad_maximum_fusion.3, f32[2,13,15]{2,1,0:T(8,128)S(1)} %pad_maximum_fusion.1), channel_id=1, replica_groups=mesh['dp'=8,'expert'=4] {'dp','expert'}, use_global_device_ids=true, to_apply=%region_33.34 | all-reduce | flops 1926 | bytes 15408 | tf_op jit(solution)/shard_map/psum | solution.py:235
  462.5 76.1 %all-reduce.6.cloned.1.call-done = (f32[384,960]{0,1:T(8,128)}, f32[384,128]{1,0:T(8,128)}, f32[960,384]{1,0:T(8,128)}, f32[13,384,15]{1,0,2:T(8,128)}, f32[13,384,15]{1,0,2:T(8,128)}) async-done(((f32[384,960]{0,1:T(8,128)}, f32[384,128]{1,0:T(8,128)}, f32[960,384]{1,0:T(8,128)}, f32[13,384,15]{1,0,2:T(8,128)}, f32[13,384,15]{1,0,2:T(8,128)}), (f32[384,960]{0,1:T(8,128)}, f32[384,128]{1,0:T(8,128)}, ...) | async-done | bytes 3744784 | tf_op jit(solution)/shard_map/psum | solution.py:235
  541.2 1.8 copy.318
  543.0 1.8 copy.319
  544.8 296.7 %all-reduce.8.cloned.1.call-done = (bf16[4,384,1536]{2,1,0:T(8,128)(2,1)}, bf16[4,1536,384]{2,1,0:T(8,128)(2,1)}) async-done(((bf16[4,384,1536]{2,1,0:T(8,128)(2,1)}, bf16[4,1536,384]{2,1,0:T(8,128)(2,1)}), (bf16[4,384,1536]{2,1,0:T(8,128)(2,1)}, bf16[4,1536,384]{2,1,0:T(8,128)(2,1)})) %all-reduce.8.cloned.1.call-update) | async-done | bytes 9437200 | tf_op jit(solution)/shard_map/psum | solution.py:249
  841.5 7.6 convert_element_type.191
  849.0 4.4 convert_element_type.193
  (247 shorter events, 43.8 us)
Async XLA Ops:
  7.2 49.8 %copy-start = (bf16[960,384]{1,0:T(8,128)(2,1)S(1)}, bf16[960,384]{1,0:T(8,128)(2,1)}, u32[]{:S(2)}) copy-start(bf16[960,384]{1,0:T(8,128)(2,1)} %param.24) | copy-start | bytes 2211844
  8.8 10.7 %copy-start.59 = (s32[2,256,4]{1,2,0:T(4,128)S(1)}, s32[2,256,4]{1,2,0:T(4,128)}, u32[]{:S(2)}) copy-start(s32[2,256,4]{1,2,0:T(4,128)} %param.17) | copy-start | bytes 24580
  9.0 10.7 %copy-start.42 = (bf16[384,64]{0,1:T(8,128)(2,1)S(1)}, bf16[384,64]{0,1:T(8,128)(2,1)}, u32[]{:S(2)}) copy-start(bf16[384,64]{0,1:T(8,128)(2,1)} %param.22) | copy-start | bytes 147460
  9.0 10.7 %copy-start.43 = (bf16[384,64]{0,1:T(8,128)(2,1)S(1)}, bf16[384,64]{0,1:T(8,128)(2,1)}, u32[]{:S(2)}) copy-start(bf16[384,64]{0,1:T(8,128)(2,1)} %param.23) | copy-start | bytes 147460
  11.6 1.4 copy-start.44
  13.0 24.7 %copy-start.35 = (f32[384]{0:T(512)}, f32[384]{0:T(512)S(1)}, u32[]{:S(2)}) copy-start(f32[384]{0:T(512)S(1)} %get-tuple-element.148) | copy-start | bytes 4612
  13.0 52.2 %copy-start.50 = (f32[384]{0:T(512)}, f32[384]{0:T(512)S(1)}, u32[]{:S(2)}) copy-start(f32[384]{0:T(512)S(1)} %get-tuple-element.149) | copy-start | bytes 4612
  19.7 27.3 %copy-start.15 = (s32[2,256,4]{2,1,0:T(8,128)}, s32[2,256,4]{2,1,0:T(8,128)S(1)}, u32[]{:S(2)}) copy-start(s32[2,256,4]{2,1,0:T(8,128)S(1)} %copy.266) | copy-start | bytes 24580
  19.7 13.8 %copy-start.24 = (bf16[384,128]{0,1:T(8,128)(2,1)}, bf16[384,128]{0,1:T(8,128)(2,1)S(1)}, u32[]{:S(2)}) copy-start(bf16[384,128]{0,1:T(8,128)(2,1)S(1)} %constant_dynamic-update-slice_fusion) | copy-start | bytes 294916
  28.8 6.2 copy-start.8
  33.5 4.2 copy-start.1
  34.9 2.8 copy-start.2
  35.0 3.0 copy-start.61
  35.0 3.0 copy-start.65
  37.7 9.3 %copy-start.67 = (f32[2,1024,64]{2,1,0:T(8,128)}, f32[2,1024,64]{2,1,0:T(8,128)S(1)}, u32[]{:S(2)}) copy-start(f32[2,1024,64]{2,1,0:T(8,128)S(1)} %fusion.27) | copy-start | bytes 1572868
  46.8 10.1 %copy-start.10 = (f32[2,256,4]{2,1,0:T(8,128)}, f32[2,256,4]{2,1,0:T(8,128)S(1)}, u32[]{:S(2)}) copy-start(f32[2,256,4]{2,1,0:T(8,128)S(1)} %get-tuple-element.138) | copy-start | bytes 24580
  46.8 207.7 %copy-start.46 = (f32[2,256]{1,0:T(2,128)}, f32[2,256]{1,0:T(2,128)S(1)}, u32[]{:S(2)}) copy-start(f32[2,256]{1,0:T(2,128)S(1)} %get-tuple-element.137) | copy-start | bytes 6148
  47.0 9.9 %copy-start.27 = (f32[2,256,4]{2,1,0:T(8,128)}, f32[2,256,4]{2,1,0:T(8,128)S(1)}, u32[]{:S(2)}) copy-start(f32[2,256,4]{2,1,0:T(8,128)S(1)} %broadcast_divide_fusion) | copy-start | bytes 24580
  59.0 11.8 %copy-start.41 = (f32[512]{0:T(512)}, f32[512]{0:T(512)S(1)}, u32[]{:S(2)}) copy-start(f32[512]{0:T(512)S(1)} %broadcast_multiply_fusion.1) | copy-start | bytes 6148
  59.8 10.9 %copy-start.51 = (f32[512]{0:T(512)}, f32[512]{0:T(512)S(1)}, u32[]{:S(2)}) copy-start(f32[512]{0:T(512)S(1)} %fusion.86) | copy-start | bytes 6148
  70.8 17.0 %copy-start.6 = (bf16[2,256,384]{2,1,0:T(8,128)(2,1)S(1)}, bf16[2,256,384]{2,1,0:T(8,128)(2,1)}, u32[]{:S(2)}) copy-start(bf16[2,256,384]{2,1,0:T(8,128)(2,1)} %param.29) | copy-start | bytes 1179652
  83.2 41.7 %all-to-all-start = ((bf16[4,1024,384]{2,1,0:T(8,128)(2,1)}), bf16[4,1024,384]{2,1,0:T(8,128)(2,1)}, u32[]{:S(2)}, u32[]{:S(2)}) async-start(bf16[4,1024,384]{2,1,0:T(8,128)(2,1)} %bitcast.199), calls=%async_computation | async-start | bytes 6291456 | tf_op jit(solution)/shard_map/all_to_all | solution.py:117
  87.8 7.1 copy-start.66
  87.9 7.6 copy-start.29
  95.6 29.3 %copy-start.37 = (f32[512]{0:T(512)}, f32[512]{0:T(512)S(1)}, u32[]{:S(2)}) copy-start(f32[512]{0:T(512)S(1)} %reduce_max.29) | copy-start | bytes 6148
  95.6 158.3 %copy-start.48 = (f32[512]{0:T(512)}, f32[512]{0:T(512)S(1)}, u32[]{:S(2)}) copy-start(f32[512]{0:T(512)S(1)} %fusion.99) | copy-start | bytes 6148
  95.8 29.0 %copy-start.17 = (f32[512,4]{1,0:T(8,128)}, f32[512,4]{1,0:T(8,128)S(1)}, u32[]{:S(2)}) copy-start(f32[512,4]{1,0:T(8,128)S(1)} %copy.279) | copy-start | bytes 24580
  124.8 41.8 %all-to-all-start.2 = ((bf16[4,1024,384]{2,1,0:T(8,128)(2,1)}), bf16[4,1024,384]{2,1,0:T(8,128)(2,1)}, u32[]{:S(2)}, u32[]{:S(2)}) async-start(bf16[4,1024,384]{2,1,0:T(8,128)(2,1)} %bitcast.201), calls=%async_computation.2 | async-start | bytes 6291456 | tf_op jit(solution)/shard_map/all_to_all | solution.py:142
  206.6 41.7 %all-to-all-start.3 = ((bf16[4,1024,384]{2,1,0:T(8,128)(2,1)}), bf16[4,1024,384]{2,1,0:T(8,128)(2,1)}, u32[]{:S(2)}, u32[]{:S(2)}) async-start(bf16[4,1024,384]{2,1,0:T(8,128)(2,1)} %bitcast.202), calls=%async_computation.3 | async-start | bytes 6291456 | tf_op jit(solution)/shard_map/all_to_all | solution.py:157
  248.3 41.6 %all-to-all-start.1 = ((bf16[4,1024,384]{2,1,0:T(8,128)(2,1)}), bf16[4,1024,384]{2,1,0:T(8,128)(2,1)}, u32[]{:S(2)}, u32[]{:S(2)}) async-start(bf16[4,1024,384]{2,1,0:T(8,128)(2,1)} %bitcast.200), calls=%async_computation.1 | async-start | bytes 6291456 | tf_op jit(solution)/shard_map/all_to_all | solution.py:127
  252.9 134.0 %reduce-scatter.2.cloned.1.call-start = ((), (), s32[]{:S(2)}) async-start(), calls=%async_computation.5 | async-start | bytes 655360 | tf_op jit(solution)/shard_map/reduce_scatter | solution.py:201
  301.1 11.8 %copy-start.38 = (f32[512]{0:T(512)S(1)}, f32[512]{0:T(512)}, u32[]{:S(2)}) copy-start(f32[512]{0:T(512)} %copy-done.37) | copy-start | bytes 6148
  301.1 12.5 %copy-start.49 = (f32[512]{0:T(512)S(1)}, f32[512]{0:T(512)}, u32[]{:S(2)}) copy-start(f32[512]{0:T(512)} %copy-done.48) | copy-start | bytes 6148
  315.1 6.6 copy-start.30
  320.6 9.2 %copy-start.16 = (s32[2,256,4]{2,1,0:T(8,128)S(1)}, s32[2,256,4]{2,1,0:T(8,128)}, u32[]{:S(2)}) copy-start(s32[2,256,4]{2,1,0:T(8,128)} %copy-done.15) | copy-start | bytes 24580
  320.6 9.2 %copy-start.28 = (f32[2,256,4]{2,1,0:T(8,128)S(1)}, f32[2,256,4]{2,1,0:T(8,128)}, u32[]{:S(2)}) copy-start(f32[2,256,4]{2,1,0:T(8,128)} %copy-done.27) | copy-start | bytes 24580
  320.6 12.7 %copy-start.52 = (f32[512]{0:T(512)}, f32[512]{0:T(512)S(1)}, u32[]{:S(2)}) copy-start(f32[512]{0:T(512)S(1)} %negate_multiply_fusion.1) | copy-start | bytes 6148
  329.8 3.6 copy-start.9
  329.8 8.4 slice-start
  333.4 4.9 slice-start.1
  343.1 3.1 copy-start.31
  343.1 3.3 copy-start.11
  343.1 3.3 copy-start.58
  343.1 3.5 copy-start.47
  346.9 16.1 %copy-start.22 = (bf16[2,1024,64]{1,2,0:T(8,128)(2,1)S(1)}, bf16[2,1024,64]{1,2,0:T(8,128)(2,1)}, u32[]{:S(2)}) copy-start(bf16[2,1024,64]{1,2,0:T(8,128)(2,1)} %fusion.45) | copy-start | bytes 786436
  352.3 13.3 %copy-start.62 = (s32[2]{0:T(128)S(1)}, s32[2]{0:T(128)}, u32[]{:S(2)}) copy-start(s32[2]{0:T(128)} %param.16) | copy-start | bytes 28
  352.4 15.7 %copy-start.12 = (bf16[512,960]{1,0:T(8,128)(2,1)S(1)}, bf16[512,960]{1,0:T(8,128)(2,1)}, u32[]{:S(2)}) copy-start(bf16[512,960]{1,0:T(8,128)(2,1)} %reshape.497) | copy-start | bytes 2949124
  352.4 15.7 %copy-start.14 = (bf16[512,384]{1,0:T(8,128)(2,1)S(1)}, bf16[512,384]{1,0:T(8,128)(2,1)}, u32[]{:S(2)}) copy-start(bf16[512,384]{1,0:T(8,128)(2,1)} %copy-done.13) | copy-start | bytes 1179652
  364.7 173.8 %all-reduce.6.cloned.1.call-start = ((), (), s32[]{:S(2)}) async-start(), calls=%async_computation.6 | async-start | bytes 7766016 | tf_op jit(solution)/shard_map/psum | solution.py:235
  388.8 452.7 %all-reduce.8.cloned.1.call-start = ((), (), s32[]{:S(2)}) async-start(), calls=%async_computation.7 | async-start | bytes 18874368 | tf_op jit(solution)/shard_map/psum | solution.py:249
  412.2 1.2 copy-start.32
  412.2 2.4 copy-start.23
  412.2 5.2 copy-start.26
  412.2 5.3 copy-start.3
  412.2 5.3 copy-start.25
  412.2 5.3 copy-start.36
  412.3 5.3 copy-start.40
  412.3 7.2 copy-start.56
  412.3 7.2 copy-start.45
  412.3 48.9 %copy-start.5 = (f32[512,384]{1,0:T(8,128)S(1)}, f32[512,384]{1,0:T(8,128)}, u32[]{:S(2)}) copy-start(f32[512,384]{1,0:T(8,128)} %copy-done.4) | copy-start | bytes 2359300
  412.3 48.8 %copy-start.53 = (f32[512]{0:T(512)S(1)}, f32[512]{0:T(512)}, u32[]{:S(2)}) copy-start(f32[512]{0:T(512)} %copy-done.52) | copy-start | bytes 6148
  841.5 7.6 copy-start.7
  849.0 4.4 copy-start.21
  849.0 5.5 copy-start.20
  (13 other events, 10.7 us)
Sparse Core Ops, SparseCore 0:
  364.9 21.9 reduce-scatter.1
  395.6 142.8 all-reduce.5
  543.1 298.3 all-reduce.7
where the time goes:
time: 869 us; the launch traced here: 862 us
  waiting for transfers between devices  459 us (53%)
  matrix products  149 us (17%)
  local copies, waits for them, and re-layouts  99.2 us (11%)
  other arithmetic  72.7 us (8%)
  blocking collectives  48.6 us (6%)
  starting transfers between devices  18.9 us (2%)
  between operations  15.2 us (2%)
    psum x1, waiting for transfers between devices, body(): lax.psum(grad_expand.astype(jnp.bfloat16), 'dp').astype(jnp.float32)  297 us
    psum x1, waiting for transfers between devices, body(): lax.psum((grad_query, grad_key_value, grad_output, grad_attend_router, gr...  76.1 us
    psum x1, blocking collectives, body(): lax.psum((grad_query, grad_key_value, grad_output, grad_attend_router, gr...  40 us
    dot_general x1, matrix products, body(): jnp.einsum('nscd,sfd->nscf', grad_produced, reduce_weight, preferred_elem...  27 us
    all_to_all x1, waiting for transfers between devices, body(): lax.all_to_all(grad_rows, 'expert', split_axis=0, concat_axis=0, tiled=True)  23.9 us
    dot_general x1, matrix products, body(): jnp.einsum('nscd,sdf->nscf', received, expand_weight, preferred_element_t...  19.9 us
  transfers between devices with their start and end apart: 7, of which 7 were waited for; matrix products, arithmetic and copies ran while one was open for 14% of the time, Pallas kernels for 0%

commit v1 on v0

--- a/solution.py
+++ b/solution.py
@@ -1,6 +1,8 @@
 import jax
 import jax.numpy as jnp
 from jax import lax
+from jax.experimental import pallas as pl
+from jax.experimental.pallas import tpu as pltpu
 from jax.sharding import PartitionSpec as P
 
 CAP = 256
@@ -24,6 +26,415 @@
 
 def activate(value):
     return jax.nn.gelu(value, approximate=True)
+
+
+F32 = jnp.float32
+LOW = jnp.bfloat16
+MESH = pl.DeviceIdType.MESH
+MIB = 2**20
+
+
+def dot(a, b):
+    return jnp.dot(a, b, preferred_element_type=F32)
+
+
+def dot_nt(a, b):
+    return lax.dot_general(a, b, (((1,), (1,)), ((), ())), preferred_element_type=F32)
+
+
+def gelu_parts(value):
+    square = value * value
+    inner = value * (0.7978845608028654 + 0.035677408136300125 * square)
+    half = 0.5 + 0.5 * jnp.tanh(inner)
+    act = value * half
+    slope = half + act * (1.0 - half) * (1.5957691216057308 + 0.2140644488178007 * square)
+    return act, slope
+
+
+def expert_kernel(
+    x_ref, c_ref, m_ref, we_hbm, wr_hbm,
+    fin_ref, grn_ref, dg_ref, gout,
+    xa, ca, ma, we, wr, xr, gp, xrt, gpt, cr, act, gh, pr, gr, ra, rb, rt2, rc, rx, dgs,
+    wsem, xs, xv, cs, cv, ms, mv, gs, gv, s1s, s1r, s2s, s2r, s3s, ys, yr, ls, k1s, k1r, k2s, k2r,
+):
+    dp = lax.axis_index("dp")
+    ex = lax.axis_index("expert")
+    y = lax.rem(dp, 2)
+    z = lax.div(dp, 2)
+    is_end = (z == 0) | (z == 3)
+    is_mid = (z == 1) | (z == 2)
+    toward = jnp.where(z < 2, dp + 2, dp - 2)
+    outer = jnp.where(z == 1, dp - 2, jnp.where(z == 2, dp + 2, dp))
+    chunks = ra.shape[0]
+    per_slot = chunks // 2
+    rows = CAP
+
+    def peer(r):
+        return (dp ^ (r // 4), ex ^ (r % 4))
+
+    def group(r):
+        return 2 * (ex ^ (r % 4)) + (y ^ (r // 4))
+
+    def remote(src, dst, send, recv, device):
+        return pltpu.make_async_remote_copy(
+            src_ref=src, dst_ref=dst, send_sem=send, recv_sem=recv,
+            device_id=device, device_id_type=MESH,
+        )
+
+    barrier = pltpu.get_barrier_semaphore()
+    for r in range(1, 8):
+        pl.semaphore_signal(barrier, 1, device_id=peer(r), device_id_type=MESH)
+    pl.semaphore_signal(barrier, 1, device_id=(toward, ex), device_id_type=MESH)
+
+    @pl.when(is_mid)
+    def _():
+        pl.semaphore_signal(barrier, 1, device_id=(outer, ex), device_id_type=MESH)
+
+    loads = []
+    for j in range(2):
+        loads.append(pltpu.make_async_copy(we_hbm.at[y * 2 + j], we.at[j], wsem.at[2 * j]))
+        loads.append(pltpu.make_async_copy(wr_hbm.at[y * 2 + j], wr.at[j], wsem.at[2 * j + 1]))
+    for load in loads:
+        load.start()
+    xa[0] = x_ref[...]
+    ca[0] = c_ref[...]
+    ma[0] = m_ref[group(0)]
+
+    pl.semaphore_wait(barrier, jnp.where(is_mid, 9, 8))
+
+    def gather_copies(r):
+        device = peer(r)
+        return (
+            remote(xa.at[0], xa.at[r], xs.at[r], xv.at[r], device),
+            remote(ca.at[0], ca.at[r], cs.at[r], cv.at[r], device),
+        )
+
+    def meta_copy(r):
+        return remote(m_ref.at[group(r)], ma.at[r], ms.at[r], mv.at[r], peer(r))
+
+    def forward_copies(r):
+        device = peer(1)
+        return (
+            remote(xa.at[r], xa.at[r + 1], xs.at[r + 1], xv.at[r + 1], device),
+            remote(ca.at[r], ca.at[r + 1], cs.at[r + 1], cv.at[r + 1], device),
+        )
+
+    direct = (1, 2, 4, 6)
+    sent = [copy for r in direct for copy in gather_copies(r)]
+    sent += [meta_copy(r) for r in range(1, 8)]
+    for copy in sent:
+        copy.start()
+    for load in loads:
+        load.wait()
+
+    def s1(c):
+        return remote(ra.at[c], rb.at[c], s1s.at[c], s1r.at[c], (toward, ex))
+
+    def s2(c):
+        return remote(rb.at[c], rt2.at[c], s2s.at[c], s2r.at[c], (toward, ex))
+
+    def s3(c):
+        return remote(ra.at[c], rt2.at[c], s3s.at[c], s2r.at[c], (outer, ex))
+
+    def out_index(c):
+        return y * chunks + c
+
+    def to_pair(src, c):
+        return remote(src.at[c], gout.at[out_index(c)], ys.at[c], yr.at[c], (dp ^ 1, ex))
+
+    def to_own(src, c):
+        return pltpu.make_async_copy(src.at[c], gout.at[out_index(c)], ls.at[c])
+
+    def tick(t):
+        @pl.when(is_mid & (t < chunks))
+        def _():
+            s1(t).wait_recv()
+            rb[t] = (ra[t].astype(F32) + rb[t].astype(F32)).astype(LOW)
+            s2(t).start()
+
+        u = jnp.maximum(t - 1, 0)
+
+        @pl.when(is_mid & (t >= 1) & (t < chunks + 1))
+        def _():
+            s2(u).wait_recv()
+            ra[u] = (rb[u].astype(F32) + rt2[u].astype(F32)).astype(LOW)
+            s3(u).start()
+            to_pair(ra, u).start()
+            to_own(ra, u).start()
+
+        w = jnp.maximum(t - 2, 0)
+
+        @pl.when(is_end & (t >= 2) & (t < chunks + 2))
+        def _():
+            s2(w).wait_recv()
+            to_pair(rt2, w).start()
+            to_own(rt2, w).start()
+
+    sub = lax.broadcasted_iota(jnp.int32, (rows, 2 * rows), 0).astype(F32)
+    lane = lax.broadcasted_iota(jnp.int32, (2 * rows, rows), 1).astype(F32)
+
+    def step(it, carry):
+        j = lax.div(it, 4)
+        s = lax.rem(it, 4)
+
+        @pl.when(it == 0)
+        def _():
+            for copy in gather_copies(1):
+                copy.wait_recv()
+            meta_copy(1).wait_recv()
+
+        @pl.when(it == 1)
+        def _():
+            for r in (2, 4, 6):
+                for copy in gather_copies(r):
+                    copy.wait_recv()
+                for copy in forward_copies(r):
+                    copy.start()
+            for r in (3, 5, 7):
+                for copy in gather_copies(r):
+                    copy.wait_recv()
+            for r in range(2, 8):
+                meta_copy(r).wait_recv()
+
+        for i in range(2):
+            r = 2 * s + i
+            hit = sub == ma[r, pl.ds(j, 1), :]
+            pick = jnp.where(hit, 1.0, 0.0).astype(LOW)
+            gate = jnp.sum(jnp.where(hit, ma[r, pl.ds(j + 2, 1), :], 0.0), 1, keepdims=True)
+            at = pl.ds(pl.multiple_of(r * rows, rows), rows)
+            x_rows = dot(pick, xa[r])
+            xr[at, :] = x_rows.astype(LOW)
+            xrt[:, at] = x_rows.T.astype(LOW)
+            c_rows = dot(pick, ca[r])
+            cr[i * rows:(i + 1) * rows, :] = c_rows.astype(LOW)
+            g_rows = gate * c_rows
+            gp[at, :] = g_rows.astype(LOW)
+            gpt[:, at] = g_rows.T.astype(LOW)
+
+        both = pl.ds(pl.multiple_of(s * 2 * rows, 2 * rows), 2 * rows)
+        x_rows = xr[both, :]
+        g_rows = gp[both, :]
+        width = 512
+        for f in range(act.shape[1] // width):
+            cols = slice(f * width, (f + 1) * width)
+            value, slope = gelu_parts(dot(x_rows, we[j, :, cols]))
+            act[both, cols] = value.astype(LOW)
+            gh[both, cols] = (dot_nt(g_rows, wr[j, cols, :]) * slope).astype(LOW)
+        made = dot(act[both, :], wr[j]).astype(LOW)
+        pr[j, both, :] = made
+        gr[j, both, :] = dot_nt(gh[both, :], we[j]).astype(LOW)
+        inner = jnp.sum(made.astype(F32) * cr[...].astype(F32), 1, keepdims=True)
+        for i in range(2):
+            r = 2 * s + i
+            hit = sub == ma[r, pl.ds(j, 1), :]
+            part = jnp.sum(jnp.where(hit, inner[i * rows:(i + 1) * rows], 0.0), 0, keepdims=True)
+            dgs[r, j] = jnp.broadcast_to(part, (8, 2 * rows))
+
+        @pl.when(s == 3)
+        def _():
+            def grads(f, carry):
+                cols = pl.ds(pl.multiple_of(f * 256, 256), 256)
+                first = j * per_slot + f
+                ra[first] = dot(gpt[...], act[:, cols]).astype(LOW)
+                second = first + per_slot // 2
+                ra[second] = dot(xrt[...], gh[:, cols]).astype(LOW)
+
+                @pl.when(is_end)
+                def _():
+                    s1(first).start()
+                    s1(second).start()
+
+                return carry
+
+            lax.fori_loop(0, per_slot // 2, grads, 0)
+
+        @pl.when(it >= 5)
+        def _():
+            tick(it - 5)
+
+        return carry
+
+    lax.fori_loop(0, 8, step, 0)
+
+    def gate_copy(r):
+        return remote(dgs.at[r], dg_ref.at[group(0)], gs.at[r], gv.at[r], peer(r))
+
+    for r in range(1, 8):
+        gate_copy(r).start()
+    dg_ref[group(0)] = dgs[0]
+
+    def block(r):
+        return act.at[pl.ds(pl.multiple_of(r * rows, rows), rows), :]
+
+    def k1(r):
+        return remote(block(r), rc.at[lax.div(r, 2)], k1s.at[lax.div(r, 2)], k1r.at[lax.div(r, 2)], peer(1))
+
+    def k2(r):
+        q = lax.div(r, 2)
+        return remote(block(r), rx.at[q], k2s.at[q], k2r.at[q], (dp ^ lax.div(r, 4), ex ^ lax.rem(r, 4)))
+
+    def combine(q, carry):
+        r = jnp.where(q < 4, 7 - 2 * q, 14 - 2 * q)
+        meta = ma[r].T
+        at = pl.ds(pl.multiple_of(r * rows, rows), rows)
+        fin = jnp.zeros((2 * rows, x_ref.shape[1]), F32)
+        grn = jnp.zeros((2 * rows, x_ref.shape[1]), F32)
+        for j in range(2):
+            hit = lane == meta[:, j:j + 1]
+            fin = fin + dot(jnp.where(hit, meta[:, 2 + j:3 + j], 0.0).astype(LOW), pr[j, at, :])
+            grn = grn + dot(jnp.where(hit, 1.0, 0.0).astype(LOW), gr[j, at, :])
+        d = x_ref.shape[1]
+        act[at, 0:d] = fin[:rows].astype(LOW)
+        act[at, d:2 * d] = fin[rows:].astype(LOW)
+        act[at, 2 * d:3 * d] = grn[:rows].astype(LOW)
+        act[at, 3 * d:4 * d] = grn[rows:].astype(LOW)
+
+        @pl.when(q < 4)
+        def _():
+            k1(r).start()
+
+        @pl.when(q >= 4)
+        def _():
+            h = lax.div(r, 2)
+            k1(r).wait_recv()
+            act[at, :] = (act[at, :].astype(F32) + rc[h].astype(F32)).astype(LOW)
+
+            @pl.when(r > 0)
+            def _():
+                k2(r).start()
+
+        tick(q + 3)
+        return carry
+
+    lax.fori_loop(0, 8, combine, 0)
+    for r in (2, 4, 6):
+        k2(r).wait_recv()
+    total = act[0:rows, :].astype(F32) + rx[1].astype(F32) + rx[2].astype(F32) + rx[3].astype(F32)
+    d = x_ref.shape[1]
+    fin_ref[0:rows, :] = total[:, 0:d]
+    fin_ref[rows:2 * rows, :] = total[:, d:2 * d]
+    grn_ref[0:rows, :] = total[:, 2 * d:3 * d]
+    grn_ref[rows:2 * rows, :] = total[:, 3 * d:4 * d]
+
+    def rest(t, carry):
+        tick(t)
+        return carry
+
+    lax.fori_loop(11, chunks + 2, rest, 0)
+
+    for copy in sent:
+        copy.wait_send()
+    for r in (2, 4, 6):
+        for copy in forward_copies(r):
+            copy.wait_send()
+        k2(r).wait_send()
+    for r in (1, 3, 5, 7):
+        k1(r).wait_send()
+    for r in range(1, 8):
+        gate_copy(r).wait_send()
+        gate_copy(r).wait_recv()
+
+    def finish(c, carry):
+        @pl.when(is_end)
+        def _():
+            s1(c).wait_send()
+            to_pair(rt2, c).wait_send()
+            to_own(rt2, c).wait()
+
+        @pl.when(is_mid)
+        def _():
+            s2(c).wait_send()
+            s3(c).wait_send()
+            to_pair(ra, c).wait_send()
+            to_own(ra, c).wait()
+
+        remote(ra.at[c], gout.at[(1 - y) * chunks + c], ys.at[c], yr.at[c], (dp ^ 1, ex)).wait_recv()
+        return carry
+
+    lax.fori_loop(0, chunks, finish, 0)
+
+
+def experts_call(x, c, meta, expand_weight, reduce_weight):
+    count, d = x.shape
+    ff = expand_weight.shape[2]
+    chunks = 4 * ff // 256
+    dma = pltpu.SemaphoreType.DMA
+    vmem = pl.BlockSpec(memory_space=pltpu.VMEM)
+    anywhere = pl.BlockSpec(memory_space=pl.ANY)
+    return pl.pallas_call(
+        expert_kernel,
+        name="experts",
+        out_shape=(
+            jax.ShapeDtypeStruct((count, d), F32),
+            jax.ShapeDtypeStruct((count, d), F32),
+            jax.ShapeDtypeStruct((8, 2, 8, count), F32),
+            jax.ShapeDtypeStruct((2 * chunks, d, 256), LOW),
+        ),
+        in_specs=[vmem, vmem, vmem, anywhere, anywhere],
+        out_specs=(vmem, vmem, vmem, anywhere),
+        scratch_shapes=[
+            pltpu.VMEM((8, count, d), LOW),
+            pltpu.VMEM((8, count, d), LOW),
+            pltpu.VMEM((8, 16, count), F32),
+            pltpu.VMEM((2, d, ff), LOW),
+            pltpu.VMEM((2, ff, d), LOW),
+            pltpu.VMEM((8 * CAP, d), LOW),
+            pltpu.VMEM((8 * CAP, d), LOW),
+            pltpu.VMEM((d, 8 * CAP), LOW),
+            pltpu.VMEM((d, 8 * CAP), LOW),
+            pltpu.VMEM((2 * CAP, d), LOW),
+            pltpu.VMEM((8 * CAP, ff), LOW),
+            pltpu.VMEM((8 * CAP, ff), LOW),
+            pltpu.VMEM((2, 8 * CAP, d), LOW),
+            pltpu.VMEM((2, 8 * CAP, d), LOW),
+            pltpu.VMEM((chunks, d, 256), LOW),
+            pltpu.VMEM((chunks, d, 256), LOW),
+            pltpu.VMEM((chunks, d, 256), LOW),
+            pltpu.VMEM((4, CAP, ff), LOW),
+            pltpu.VMEM((4, CAP, ff), LOW),
+            pltpu.VMEM((8, 2, 8, count), F32),
+            dma((4,)),
+            dma((8,)), dma((8,)), dma((8,)), dma((8,)), dma((8,)), dma((8,)), dma((8,)), dma((8,)),
+            dma((chunks,)), dma((chunks,)), dma((chunks,)), dma((chunks,)), dma((chunks,)),
+            dma((chunks,)), dma((chunks,)), dma((chunks,)),
+            dma((4,)), dma((4,)), dma((4,)), dma((4,)),
+        ],
+        compiler_params=pltpu.CompilerParams(
+            collective_id=0, has_side_effects=True, vmem_limit_bytes=62 * MIB
+        ),
+    )(x, c, meta, expand_weight, reduce_weight)
+
+
+def widen_kernel(r_ref, e_ref, reduce_ref, expand_ref):
+    reduce_ref[0] = r_ref[0].astype(F32).T
+    expand_ref[0] = e_ref[0].astype(F32)
+
+
+def widen_call(chunks, slots, d, ff):
+    n = ff // 256
+    return pl.pallas_call(
+        widen_kernel,
+        name="widen",
+        grid=(slots, n),
+        in_specs=[
+            pl.BlockSpec((1, d, 256), lambda s, f: (s * 2 * n + f, 0, 0)),
+            pl.BlockSpec((1, d, 256), lambda s, f: (s * 2 * n + n + f, 0, 0)),
+        ],
+        out_specs=(
+            pl.BlockSpec((1, 256, d), lambda s, f: (s, f, 0)),
+            pl.BlockSpec((1, d, 256), lambda s, f: (s, 0, f)),
+        ),
+        out_shape=(
+            jax.ShapeDtypeStruct((slots, ff, d), F32),
+            jax.ShapeDtypeStruct((slots, d, ff), F32),
+        ),
+    )(chunks, chunks)
+
+
+def masked_softmax(logits, chosen):
+    top = jnp.max(jnp.where(chosen > 0, logits, -jnp.inf), -1, keepdims=True)
+    expo = jnp.where(chosen > 0, jnp.exp(logits - top), 0.0)
+    return expo / jnp.sum(expo, -1, keepdims=True)
 
 
 def body(
@@ -269,6 +680,216 @@
     )
 
 
+def body_fast(
+    tokens,
+    task_ids,
+    attention_picks,
+    feedforward_picks,
+    norm_gain,
+    norm_bias,
+    query_weight,
+    key_weight,
+    value_weight,
+    output_weight,
+    attention_router,
+    feedforward_router,
+    expand_weight,
+    reduce_weight,
+    cotangent,
+):
+    images, patches, width = tokens.shape
+    count = images * patches
+    tasks = attention_router.shape[0]
+    experts = attention_router.shape[2]
+    head = key_weight.shape[1]
+    picks = attention_picks.shape[2]
+    slots = expand_weight.shape[0]
+    groups = lax.axis_size("expert")
+    lanes = groups * slots
+    f32 = jnp.float32
+    low_type = jnp.bfloat16
+    inputs = tokens.astype(f32).reshape(count, width)
+    expert_range = jnp.arange(experts, dtype=jnp.int32)
+    task_hot = (task_ids[:, None] == jnp.arange(tasks, dtype=jnp.int32)[None, :]).astype(f32)
+    task_low = task_hot.astype(low_type)
+    attend_hot = (attention_picks[..., None] == expert_range).astype(f32)
+    attend_low = attend_hot.astype(low_type)
+    choices = feedforward_picks.reshape(count, picks)
+    wide = jnp.arange(experts + 1, dtype=jnp.int32)
+    feed_hot = (choices[..., None] == expert_range).astype(f32)
+    chosen = jnp.sum((choices[..., None] == wide).astype(f32), 1)
+    earlier = jnp.arange(count)[:, None] > jnp.arange(count)[None, :]
+    before = jnp.dot(earlier.astype(low_type), chosen.astype(low_type), preferred_element_type=f32)
+    rank = jnp.where(chosen > 0, before, -1.0).T
+    first, first_back = jax.vjp(normalize, inputs, norm_gain[0], norm_bias[0])
+    normed_one = first.astype(low_type)
+    shaped_one = normed_one.reshape(images, patches, width)
+    router_one = jnp.einsum(
+        "it,tde->ide", task_low, attention_router, preferred_element_type=f32
+    ).astype(low_type)
+    logits_one = jnp.einsum("ipd,ide->ipe", shaped_one, router_one, preferred_element_type=f32)
+    gates_one, gates_one_back = jax.vjp(lambda value: gate_weights(value, attend_hot), logits_one)
+    queries_all = jnp.dot(normed_one, query_weight, preferred_element_type=f32).astype(low_type)
+    queries_all = queries_all.reshape(images, patches, experts, head)
+    queries = jnp.einsum(
+        "ipke,ipeh->ipkh", attend_low, queries_all, preferred_element_type=f32
+    ).astype(low_type)
+    queries = queries.reshape(images, patches * picks, head)
+    key_value = jnp.concatenate([key_weight, value_weight], 1)
+    pair = jnp.dot(normed_one, key_value, preferred_element_type=f32).astype(low_type)
+    pair = pair.reshape(images, patches, 2 * head)
+    pair_all = lax.all_gather(pair, "expert", axis=1, tiled=True)
+    keys_all = pair_all[:, :, :head]
+    values_all = pair_all[:, :, head:]
+    scores = jnp.einsum("irh,ish->irs", queries, keys_all, preferred_element_type=f32) * 0.125
+    top = jnp.max(scores, -1, keepdims=True)
+    expo = jnp.exp(scores - top)
+    total = jnp.sum(expo, -1, keepdims=True)
+    log_total = top + jnp.log(total)
+    probs_low = (expo / total).astype(low_type)
+    attended = jnp.einsum("irs,ish->irh", probs_low, values_all, preferred_element_type=f32)
+    attended = attended.reshape(images, patches, picks, head)
+    weighted = gates_one[..., None] * attended
+    heads = jnp.einsum("ipke,ipkh->ipeh", attend_hot, weighted, precision=HIGH)
+    heads = heads.reshape(count, experts * head).astype(low_type)
+    middle = inputs + jnp.dot(heads, output_weight, preferred_element_type=f32)
+    second, second_back = jax.vjp(normalize, middle, norm_gain[1], norm_bias[1])
+    normed_two = second.astype(low_type)
+    shaped_two = normed_two.reshape(images, patches, width)
+    router_two = jnp.einsum(
+        "it,tde->ide", task_low, feedforward_router, preferred_element_type=f32
+    ).astype(low_type)
+    logits_two = jnp.einsum(
+        "ipd,ide->ipe", shaped_two, router_two, preferred_element_type=f32
+    ).reshape(count, experts)
+    gates_two = masked_softmax(logits_two, chosen[:, :experts])
+    gate_rows = jnp.pad(gates_two, ((0, 0), (0, 1))).T
+    pairs = lanes // 2
+    meta = jnp.concatenate(
+        [
+            rank.reshape(pairs, 2, count),
+            gate_rows.reshape(pairs, 2, count),
+            jnp.zeros((pairs, 12, count), f32),
+        ],
+        1,
+    )
+    final_part, grad_normed_two, grad_gate_rows, grad_chunks = experts_call(
+        normed_two, cotangent.reshape(count, width), meta, expand_weight, reduce_weight
+    )
+    output = (middle + final_part).astype(low_type).reshape(images, patches, width)
+    grad_final = cotangent.astype(f32).reshape(count, width)
+    grad_gates = grad_gate_rows[:, :, 0].reshape(2 * pairs, count)[:experts].T
+    grad_logits_two = gates_two * (
+        grad_gates - jnp.sum(gates_two * grad_gates, -1, keepdims=True)
+    )
+    grad_logits_two = grad_logits_two.astype(low_type).reshape(images, patches, experts)
+    per_image_two = jnp.einsum(
+        "ipd,ipe->ide", shaped_two, grad_logits_two, preferred_element_type=f32
+    )
+    grad_feed_router = jnp.einsum("it,ide->tde", task_hot, per_image_two, precision=HIGH)
+    grad_normed_two = grad_normed_two + jnp.einsum(
+        "ipe,ide->ipd", grad_logits_two, router_two, preferred_element_type=f32
+    ).reshape(count, width)
+    grad_middle_norm, grad_gain_two, grad_bias_two = second_back(grad_normed_two)
+    grad_middle = grad_final + grad_middle_norm
+    grad_branch = grad_middle.astype(low_type)
+    grad_output = jnp.einsum("tc,td->cd", heads, grad_branch, preferred_element_type=f32)
+    grad_heads = jnp.einsum(
+        "td,cd->tc", grad_branch, output_weight, preferred_element_type=f32
+    ).astype(low_type)
+    grad_heads = grad_heads.reshape(images, patches, experts, head)
+    grad_selected = jnp.einsum(
+        "ipke,ipeh->ipkh", attend_low, grad_heads, preferred_element_type=f32
+    )
+    grad_gates_one = jnp.sum(attended * grad_selected, -1)
+    grad_attended = (
+        (gates_one[..., None] * grad_selected)
+        .astype(low_type)
+        .reshape(images, patches * picks, head)
+    )
+    scores_back = jnp.einsum("irh,ish->irs", queries, keys_all, preferred_element_type=f32) * 0.125
+    probs_back = jnp.exp(scores_back - log_total)
+    grad_values = jnp.einsum(
+        "irs,irh->ish", probs_back.astype(low_type), grad_attended, preferred_element_type=f32
+    )
+    grad_probs = jnp.einsum("irh,ish->irs", grad_attended, values_all, preferred_element_type=f32)
+    inner_sum = jnp.sum(probs_back * grad_probs, -1, keepdims=True)
+    grad_scores = (probs_back * (grad_probs - inner_sum)).astype(low_type)
+    grad_query_sel = (
+        jnp.einsum("irs,ish->irh", grad_scores, keys_all, preferred_element_type=f32) * 0.125
+    )
+    grad_keys = jnp.einsum("irs,irh->ish", grad_scores, queries, preferred_element_type=f32) * 0.125
+    grad_pair = jnp.concatenate([grad_keys, grad_values], -1)
+    pair_sum = lax.psum_scatter(
+        grad_pair.astype(jnp.bfloat16), "expert", scatter_dimension=1, tiled=True
+    ).astype(jnp.float32)
+    pair_sum = pair_sum.astype(low_type).reshape(count, 2 * head)
+    grad_query_sel = grad_query_sel.reshape(images, patches, picks, head)
+    grad_queries_all = jnp.einsum("ipke,ipkh->ipeh", attend_hot, grad_query_sel, precision=HIGH)
+    grad_queries_all = grad_queries_all.astype(low_type).reshape(count, experts * head)
+    grad_logits_one = gates_one_back(grad_gates_one)[0].astype(low_type)
+    per_image_one = jnp.einsum(
+        "ipd,ipe->ide", shaped_one, grad_logits_one, preferred_element_type=f32
+    )
+    grad_attend_router = jnp.einsum("it,ide->tde", task_hot, per_image_one, precision=HIGH)
+    grad_query = jnp.einsum("td,tc->dc", normed_one, grad_queries_all, preferred_element_type=f32)
+    grad_key_value = jnp.einsum("td,tc->dc", normed_one, pair_sum, preferred_element_type=f32)
+    grad_normed_one = jnp.einsum(
+        "tc,dc->td", grad_queries_all, query_weight, preferred_element_type=f32
+    )
+    grad_normed_one = grad_normed_one + jnp.einsum(
+        "tc,dc->td", pair_sum, key_value, preferred_element_type=f32
+    )
+    grad_normed_one = grad_normed_one + jnp.einsum(
+        "ipe,ide->ipd", grad_logits_one, router_one, preferred_element_type=f32
+    ).reshape(count, width)
+    grad_inputs_norm, grad_gain_one, grad_bias_one = first_back(grad_normed_one)
+    grad_tokens = (grad_middle + grad_inputs_norm).reshape(images, patches, width)
+    grad_gain = jnp.stack([grad_gain_one, grad_gain_two])
+    grad_bias = jnp.stack([grad_bias_one, grad_bias_two])
+    feed_shaped = feed_hot.reshape(images, patches, picks, experts)
+    usage = jnp.stack(
+        [
+            jnp.einsum("it,ipke->te", task_hot, attend_hot, precision=HIGH),
+            jnp.einsum("it,ipke->te", task_hot, feed_shaped, precision=HIGH),
+        ]
+    )
+    shared = lax.psum(
+        (
+            grad_query,
+            grad_key_value,
+            grad_output,
+            grad_attend_router,
+            grad_feed_router,
+            grad_gain,
+            grad_bias,
+            usage,
+        ),
+        ("dp", "expert"),
+    )
+    grad_reduce_sum, grad_expand_sum = widen_call(
+        grad_chunks, slots, width, expand_weight.shape[2]
+    )
+    grad_key_sum = shared[1][:, :head]
+    grad_value_sum = shared[1][:, head:]
+    return (
+        output,
+        grad_tokens,
+        shared[5],
+        shared[6][0],
+        shared[6][1],
+        shared[0],
+        grad_key_sum,
+        grad_value_sum,
+        shared[2],
+        shared[3],
+        shared[4],
+        grad_expand_sum,
+        grad_reduce_sum,
+        shared[7],
+    )
+
+
 def solution(mesh):
     placed = (
         P("dp", "expert", None),
@@ -287,8 +908,9 @@
         P("expert", None, None),
         P("dp", "expert", None),
     )
+    fast = mesh.shape["dp"] == 8 and mesh.shape["expert"] == 4
     return jax.shard_map(
-        body,
+        body_fast if fast else body,
         mesh=mesh,
         in_specs=placed,
         out_specs=(

time: 869 us -> 553 us (0.64)
  waiting for transfers between devices: 459 us -> 93.8 us
  Pallas kernels: 0 us -> 254 us
  matrix products: 149 us -> 59.1 us
  local copies, waits for them, and re-layouts: 99.2 us -> 42.1 us
  other arithmetic: 72.7 us -> 34.1 us
  starting transfers between devices: 18.9 us -> 0.08 us
    psum x2 -> x1, waiting for transfers between devices: 373 us -> 93.8 us  [body_fast(): lax.psum((grad_query, grad_key_value, grad_output, grad_attend_router, gr...]
    pallas_call x0 -> x2, Pallas kernels: none -> 254 us  [the longest x1 235 us: experts_call(): pl.pallas_call(expert_kernel, name='experts', out_shape=(jax.ShapeDtypeSt...]
    dot_general x37 -> x32, matrix products: 149 us -> 59.1 us  [the longest x1 6.43 us: body_fast(): jnp.einsum('ipke,ipkh->ipeh', attend_hot, grad_query_sel, precision=HIGH)]
    all_to_all x4 -> x0, waiting for transfers between devices: 72.2 us -> none  [the longest x1 23.9 us: body(): lax.all_to_all(grad_rows, 'expert', split_axis=0, concat_axis=0, tiled=True)]
    gather x2 -> x0, local copies, waits for them, and re-layouts: 22.7 us -> none  [the longest x1 11.6 us: body(): grad_back[position].astype(f32).reshape(count, picks, width)]
    all_to_all x4 -> x0, starting transfers between devices: 18.8 us -> none  [the longest x1 4.85 us: body(): lax.all_to_all(grad_send, 'expert', split_axis=0, concat_axis=0, tiled=True)]
    convert_element_type x6 -> x1, local copies, waits for them, and re-layouts: 17.3 us -> 3.22 us  [body_fast(): heads = heads.reshape(count, experts * head).astype(low_type)]
    reduce_scatter x1, waiting for transfers between devices: 13.9 us -> 0.01 us  [body_fast(): lax.psum_scatter(grad_pair.astype(jnp.bfloat16), 'expert', scatter_dimens...]
  transfers between devices with their start and end apart: 7 -> 2, of which waited for: 7 -> 1; matrix products, arithmetic and copies ran while one was open for 14% -> 8% of each run, Pallas kernels for 0% -> 3%
where the time goes in v1:
time: 553 us; the launch traced here: 546 us
  Pallas kernels  254 us (46%)
  waiting for transfers between devices  93.8 us (17%)
  matrix products  59.1 us (11%)
  blocking collectives  48.2 us (9%)
  local copies, waits for them, and re-layouts  42.1 us (8%)
  other arithmetic  34.1 us (6%)
  between operations  15.2 us (3%)
    pallas_call x1, Pallas kernels, experts_call(): pl.pallas_call(expert_kernel, name='experts', out_shape=(jax.ShapeDtypeSt...  235 us
    psum x1, waiting for transfers between devices, body_fast(): lax.psum((grad_query, grad_key_value, grad_output, grad_attend_router, gr...  93.8 us
    psum x1, blocking collectives, body_fast(): lax.psum((grad_query, grad_key_value, grad_output, grad_attend_router, gr...  39.5 us
    unnamed x124, local copies, waits for them, and re-layouts  18.8 us
    pallas_call x1, Pallas kernels, widen_call(): pl.pallas_call(widen_kernel, name='widen', grid=(slots, n), in_specs=[pl....  18.8 us
  transfers between devices with their start and end apart: 2, of which 1 were waited for; matrix products, arithmetic and copies ran while one was open for 8% of the time, Pallas kernels for 3%

profile of v1, /device:TPU:0, one launch (start us, length us, event | category | flops | bytes accessed | tf_op | source)
XLA Modules:
  0.0 546.2 jit_solution(13032639213968918805)
XLA Ops:
  7.3 1.2 convert_reduce_fusion.1
  8.5 1.3 multiply_reduce_fusion.8
  9.8 1.4 slice_reduce_fusion.3
  11.2 1.2 add_convert_fusion.2
  12.4 1.8 convolution_convert_fusion.3
  14.5 3.2 copy.218
  18.3 8.6 %all_gather.3 = bf16[2,1024,128]{1,2,0:T(8,128)(2,1)S(1)} all-gather(bf16[2,256,128]{1,2,0:T(8,128)(2,1)S(1)} %copy.219), channel_id=1, replica_groups=mesh['dp'=8,'expert'=4] {'expert'}, dimensions={1}, use_global_device_ids=true | all-gather | bytes 655360 | tf_op jit(solution)/shard_map/all_gather | solution.py:741
  26.9 2.6 convolution_convert_fusion.4
  29.6 0.8 copy-done.19
  30.4 1.3 multiply_reduce_fusion.1
  31.7 1.4 fusion.1
  33.1 2.7 fusion.5
  37.8 7.3 %select_reduce_fusion.1 = f32[2,256,4]{2,1,0:T(8,128)S(1)} fusion(f32[2,256,15]{2,1,0:T(8,128)S(1)} %fusion.41, s32[2,256,4]{2,1,0:T(8,128)S(1)} %copy.214), kind=kLoop, calls=%fused_computation.41 | loop fusion | flops 90112 | bytes 47104 | tf_op jit(solution)/shard_map/jvp()/reduce_sum | solution.py:23
  47.1 5.8 %convolution_convert_fusion.1 = bf16[2,256,15,64]{3,2,1,0:T(8,128)(2,1)} fusion(f32[2,256,4,64]{3,2,1,0:T(4,128)S(1)} %bitcast.142, f32[2,256,4]{2,1,0:T(8,128)S(1)} %broadcast_divide_fusion, s32[2,256,4]{2,1,0:T(8,128)S(1)} %copy.214), kind=kOutput, calls=%fused_computation.12 | convolution fusion | flops 24246272 | bytes 1523712 | tf_op jit(solution)/shard_map/ipke,ipkh->ipeh/dot_general | solution.py:753
  53.0 3.2 reshape.313
  56.2 0.8 fusion.70
  57.8 0.8 copy-done.7
  60.0 0.8 maximum_maximum_fusion.m_ref
  60.8 234.8 %experts.1 = (f32[512,384]{1,0:T(8,128)}, f32[512,384]{1,0:T(8,128)}, f32[8,2,8,512]{3,2,1,0:T(8,128)}, bf16[48,384,256]{2,1,0:T(8,128)(2,1)}) custom-call(bf16[512,384]{1,0:T(8,128)(2,1)} %copy-done.7, bf16[512,384]{1,0:T(8,128)(2,1)} %bitcast.118, f32[8,16,512]{2,1,0:T(8,128)} %maximum_maximum_fusion.m_ref, bf16[4,384,1536]{2,1,0:T(8,128)(2,1)} %we_hbm.1, ...), custom_call_target="tpu_custom_call" | custom-call | tf_op jit(solution)/shard_map/experts/pallas_call | solution.py:364
  295.6 1.0 slice_reduce_fusion
  296.7 0.8 multiply_reduce_fusion.10
  297.4 0.8 multiply_convert_fusion.2
  298.3 1.0 fusion.35
  299.3 2.2 multiply_reduce_fusion.3
  302.2 2.2 fusion.67
  304.4 1.2 fusion.20
  305.6 0.7 copy-done.16
  306.3 1.6 convolution_convert_fusion.2
  308.0 2.5 reshape.299
  310.5 3.2 copy.229
  313.7 4.4 multiply_convert_fusion.1
  318.1 5.1 fusion.8
  323.3 2.1 multiply_reduce_fusion
  325.4 2.5 multiply_convert_fusion
  327.9 2.0 copy-done.3
  329.9 1.4 fusion.11
  331.4 0.9 pad_maximum_fusion
  332.3 3.1 convolution_multiply_fusion.1
  335.6 1.3 copy.232
  336.9 6.4 %convolution_convert_fusion = bf16[2,256,15,64]{3,2,1,0:T(8,128)(2,1)} fusion(f32[2,256,4,64]{3,2,1,0:T(4,128)} %bitcast.124, s32[2,256,4]{2,1,0:T(8,128)} %copy-done.17), kind=kOutput, calls=%fused_computation.11 | convolution fusion | flops 24115200 | bytes 1515520 | tf_op jit(solution)/shard_map/ipke,ipkh->ipeh/dot_general | solution.py:828
  343.4 4.1 reshape.314
  347.5 1.2 fusion.29
  348.7 1.2 multiply_reduce_fusion.9
  349.9 1.2 add_multiply_fusion
  351.0 3.9 convert_reduce_fusion
  356.0 18.8 %widen.1 = (f32[4,1536,384]{2,1,0:T(8,128)}, f32[4,384,1536]{2,1,0:T(8,128)}) custom-call(bf16[48,384,256]{2,1,0:T(8,128)(2,1)} %get-tuple-element.23.r_ref.e_ref, bf16[48,384,256]{2,1,0:T(8,128)(2,1)} %get-tuple-element.23.r_ref.e_ref), custom_call_target="tpu_custom_call" | custom-call | tf_op jit(solution)/shard_map/widen/pallas_call | solution.py:415
  374.8 1.2 fusion.31
  376.0 1.2 fusion.39
  377.2 2.9 fusion.72
  380.1 3.0 fusion.73
  383.1 1.9 convolution_bitcast_fusion
  385.0 3.1 fusion.71
  388.2 1.0 copy.238
  389.2 2.2 fusion.66
  391.9 39.5 %all-reduce.1 = (f32[2,384]{1,0:T(2,128)}, f32[2,384]{1,0:T(2,128)S(1)}, f32[2,13,15]{2,1,0:T(8,128)S(1)}) all-reduce(f32[2,384]{1,0:T(2,128)S(1)} %pad_maximum_fusion.2, f32[2,384]{1,0:T(2,128)S(1)} %pad_maximum_fusion.3, f32[2,13,15]{2,1,0:T(8,128)S(1)} %pad_maximum_fusion.1), channel_id=1, replica_groups=mesh['dp'=8,'expert'=4] {'dp','expert'}, use_global_device_ids=true, to_apply=%region_24.25 | all-reduce | flops 1926 | bytes 15408 | tf_op jit(solution)/shard_map/psum | solution.py:857
  432.6 1.3 add_add_fusion.2
  433.9 93.8 %all-reduce.5.cloned.1.call-done = (f32[384,960]{0,1:T(8,128)}, f32[384,128]{1,0:T(8,128)}, f32[960,384]{1,0:T(8,128)}, f32[13,384,15]{1,0,2:T(8,128)}, f32[13,384,15]{1,0,2:T(8,128)}) async-done(((f32[384,960]{0,1:T(8,128)}, f32[384,128]{1,0:T(8,128)}, f32[960,384]{1,0:T(8,128)}, f32[13,384,15]{1,0,2:T(8,128)}, f32[13,384,15]{1,0,2:T(8,128)}), (f32[384,960]{0,1:T(8,128)}, f32[384,128]{1,0:T(8,128)}, ...) | async-done | bytes 3744784 | tf_op jit(solution)/shard_map/psum | solution.py:857
  527.7 1.1 fusion.68
  528.8 0.8 copy.249
  529.6 0.8 copy.250
  530.4 1.8 copy.251
  532.2 1.8 copy.252
  534.0 2.6 copy.305
  536.6 2.6 copy.306
  (172 shorter events, 10.6 us)
Async XLA Ops:
  7.2 49.0 %copy-start = (bf16[960,384]{1,0:T(8,128)(2,1)S(1)}, bf16[960,384]{1,0:T(8,128)(2,1)}, u32[]{:S(2)}) copy-start(bf16[960,384]{1,0:T(8,128)(2,1)} %param.24) | copy-start | bytes 2211844
  7.2 10.5 %copy-start.47 = (s32[2,256,4]{1,2,0:T(4,128)S(1)}, s32[2,256,4]{1,2,0:T(4,128)}, u32[]{:S(2)}) copy-start(s32[2,256,4]{1,2,0:T(4,128)} %param.17) | copy-start | bytes 24580
  7.2 10.6 %copy-start.31 = (bf16[384,64]{0,1:T(8,128)(2,1)S(1)}, bf16[384,64]{0,1:T(8,128)(2,1)}, u32[]{:S(2)}) copy-start(bf16[384,64]{0,1:T(8,128)(2,1)} %param.22) | copy-start | bytes 147460
  7.2 10.7 %copy-start.32 = (bf16[384,64]{0,1:T(8,128)(2,1)S(1)}, bf16[384,64]{0,1:T(8,128)(2,1)}, u32[]{:S(2)}) copy-start(bf16[384,64]{0,1:T(8,128)(2,1)} %param.23) | copy-start | bytes 147460
  7.2 375.9 %reduce-scatter.2.cloned.1.call-start = ((), (), s32[]{:S(2)}) async-start(), calls=%async_computation.1 | async-start | bytes 655360 | tf_op jit(solution)/shard_map/reduce_scatter | solution.py:823
  9.8 1.4 copy-start.42
  9.8 21.9 %copy-start.34 = (f32[512]{0:T(512)}, f32[512]{0:T(512)S(1)}, u32[]{:S(2)}) copy-start(f32[512]{0:T(512)S(1)} %rsqrt.24) | copy-start | bytes 6148
  9.8 1.4 copy-start.29
  17.9 28.6 %copy-start.17 = (s32[2,256,4]{2,1,0:T(8,128)}, s32[2,256,4]{2,1,0:T(8,128)S(1)}, u32[]{:S(2)}) copy-start(s32[2,256,4]{2,1,0:T(8,128)S(1)} %copy.214) | copy-start | bytes 24580
  26.9 6.2 %copy-start.9 = (bf16[2,1024,128]{1,2,0:T(8,128)(2,1)}, bf16[2,1024,128]{1,2,0:T(8,128)(2,1)S(1)}, u32[]{:S(2)}) copy-start(bf16[2,1024,128]{1,2,0:T(8,128)(2,1)S(1)} %all_gather.3) | copy-start | bytes 1572868
  29.6 0.8 copy-start.19
  31.7 4.1 copy-start.2
  33.1 2.8 copy-start.4
  33.1 3.0 copy-start.48
  33.1 3.0 copy-start.50
  35.8 10.6 %copy-start.52 = (f32[2,1024,64]{2,1,0:T(8,128)}, f32[2,1024,64]{2,1,0:T(8,128)S(1)}, u32[]{:S(2)}) copy-start(f32[2,1024,64]{2,1,0:T(8,128)S(1)} %fusion.5) | copy-start | bytes 1572868
  36.1 0.8 copy-start.5
  36.9 0.6 copy-start.27
  37.8 19.5 %copy-start.51 = (bf16[13,384,15]{1,2,0:T(8,128)(2,1)S(1)}, bf16[13,384,15]{1,2,0:T(8,128)(2,1)}, u32[]{:S(2)}) copy-start(bf16[13,384,15]{1,2,0:T(8,128)(2,1)} %param.26) | copy-start | bytes 449284
  37.8 19.7 %copy-start.33 = (f32[384]{0:T(512)S(1)}, f32[384]{0:T(512)}, u32[]{:S(2)}) copy-start(f32[384]{0:T(512)} %get-tuple-element.157) | copy-start | bytes 4612
  37.8 19.7 %copy-start.44 = (f32[384]{0:T(512)S(1)}, f32[384]{0:T(512)}, u32[]{:S(2)}) copy-start(f32[384]{0:T(512)} %get-tuple-element.123) | copy-start | bytes 4612
  45.6 0.7 copy-start.11
  45.6 12.2 %copy-start.36 = (f32[2,256]{1,0:T(2,128)}, f32[2,256]{1,0:T(2,128)S(1)}, u32[]{:S(2)}) copy-start(f32[2,256]{1,0:T(2,128)S(1)} %get-tuple-element.149) | copy-start | bytes 6148
  46.4 0.7 copy-start.22
  47.1 11.7 %copy-start.39 = (s32[1,1,512,4]{2,3,1,0:T(4,128)S(1)}, s32[1,1,512,4]{2,3,1,0:T(4,128)}, u32[]{:S(2)}) copy-start(s32[1,1,512,4]{2,3,1,0:T(4,128)} %param.18) | copy-start | bytes 24580
  56.2 2.6 copy-start.13
  57.3 3.5 copy-start.41
  57.3 3.5 copy-start.38
  57.5 3.3 copy-start.26
  57.8 0.8 copy-start.7
  59.2 0.6 copy-start.21
  298.2 3.9 copy-start.24
  304.4 9.3 %copy-start.18 = (s32[2,256,4]{2,1,0:T(8,128)S(1)}, s32[2,256,4]{2,1,0:T(8,128)}, u32[]{:S(2)}) copy-start(s32[2,256,4]{2,1,0:T(8,128)} %copy-done.17) | copy-start | bytes 24580
  304.4 9.3 %copy-start.23 = (f32[2,256,4]{2,1,0:T(8,128)S(1)}, f32[2,256,4]{2,1,0:T(8,128)}, u32[]{:S(2)}) copy-start(f32[2,256,4]{2,1,0:T(8,128)} %copy-done.22) | copy-start | bytes 24580
  305.6 0.7 copy-start.16
  313.7 9.6 %slice-start = ((s8[8388608]{0:T(1024)(128)(4,1)}), s8[4194304]{0:T(1024)(128)(4,1)S(1)}, s32[]{:S(2)}) async-start(s8[8388608]{0:T(1024)(128)(4,1)} %bitcast.112), calls=%async_computation.3 | async-start | bytes 8388608
  313.7 9.6 %copy-start.10 = (bf16[2,1024,128]{1,2,0:T(8,128)(2,1)S(1)}, bf16[2,1024,128]{1,2,0:T(8,128)(2,1)}, u32[]{:S(2)}) copy-start(bf16[2,1024,128]{1,2,0:T(8,128)(2,1)} %copy-done.9) | copy-start | bytes 1572868
  318.1 5.2 slice-start.1
  325.4 4.5 copy-start.20
  327.9 2.0 copy-start.3
  329.9 5.5 %copy-start.8 = (bf16[512,384]{1,0:T(8,128)(2,1)S(1)}, bf16[512,384]{1,0:T(8,128)(2,1)}, u32[]{:S(2)}) copy-start(bf16[512,384]{1,0:T(8,128)(2,1)} %copy-done.7) | copy-start | bytes 1179652
  329.9 5.5 %copy-start.25 = (bf16[2,256,15]{1,0,2:T(2,128)(2,1)S(1)}, bf16[2,256,15]{1,0,2:T(2,128)(2,1)}, u32[]{:S(2)}) copy-start(bf16[2,256,15]{1,0,2:T(2,128)(2,1)} %copy-done.24) | copy-start | bytes 46084
  329.9 5.7 %copy-start.37 = (f32[2,256]{1,0:T(2,128)S(1)}, f32[2,256]{1,0:T(2,128)}, u32[]{:S(2)}) copy-start(f32[2,256]{1,0:T(2,128)} %copy-done.36) | copy-start | bytes 6148
  331.3 16.1 %copy-start.49 = (s32[2]{0:T(128)S(1)}, s32[2]{0:T(128)}, u32[]{:S(2)}) copy-start(s32[2]{0:T(128)} %param.16) | copy-start | bytes 28
  331.3 17.3 %copy-start.12 = (f32[2,256,4]{2,1,0:T(8,128)S(1)}, f32[2,256,4]{2,1,0:T(8,128)}, u32[]{:S(2)}) copy-start(f32[2,256,4]{2,1,0:T(8,128)} %copy-done.11) | copy-start | bytes 24580
  332.2 22.8 %copy-start.6 = (bf16[2,256,384]{2,1,0:T(8,128)(2,1)S(1)}, bf16[2,256,384]{2,1,0:T(8,128)(2,1)}, u32[]{:S(2)}) copy-start(bf16[2,256,384]{2,1,0:T(8,128)(2,1)} %copy-done.5) | copy-start | bytes 1179652
  332.2 23.0 %copy-start.46 = (f32[384]{0:T(512)S(1)}, f32[384]{0:T(512)}, u32[]{:S(2)}) copy-start(f32[384]{0:T(512)} %get-tuple-element.116) | copy-start | bytes 4612
  332.3 23.0 %copy-start.45 = (f32[384]{0:T(512)S(1)}, f32[384]{0:T(512)}, u32[]{:S(2)}) copy-start(f32[384]{0:T(512)} %get-tuple-element.110) | copy-start | bytes 4612
  332.3 23.3 %copy-start.40 = (s32[1,1,512,4]{2,3,1,0:T(4,128)S(1)}, s32[1,1,512,4]{2,3,1,0:T(4,128)}, u32[]{:S(2)}) copy-start(s32[1,1,512,4]{2,3,1,0:T(4,128)} %param.18) | copy-start | bytes 24580
  332.3 195.4 %all-reduce.5.cloned.1.call-start = ((), (), s32[]{:S(2)}) async-start(), calls=%async_computation.2 | async-start | bytes 7766016 | tf_op jit(solution)/shard_map/psum | solution.py:857
  356.0 20.0 %copy-start.28 = (bf16[2,384,15]{1,0,2:T(2,128)(2,1)S(1)}, bf16[2,384,15]{1,0,2:T(2,128)(2,1)}, u32[]{:S(2)}) copy-start(bf16[2,384,15]{1,0,2:T(2,128)(2,1)} %copy-done.27) | copy-start | bytes 69124
  356.0 21.2 %copy-start.14 = (bf16[512,960]{1,0:T(8,128)(2,1)S(1)}, bf16[512,960]{1,0:T(8,128)(2,1)}, u32[]{:S(2)}) copy-start(bf16[512,960]{1,0:T(8,128)(2,1)} %copy-done.13) | copy-start | bytes 2949124
  374.8 14.4 %copy-start.30 = (f32[1,2,2,128]{3,1,2,0:T(2,128)S(1)}, f32[1,2,2,128]{3,1,2,0:T(2,128)}, u32[]{:S(2)}) copy-start(f32[1,2,2,128]{3,1,2,0:T(2,128)} %copy-done.29) | copy-start | bytes 6148
  376.0 15.4 %copy-start.43 = (f32[1,2,2,128]{3,1,2,0:T(2,128)S(1)}, f32[1,2,2,128]{3,1,2,0:T(2,128)}, u32[]{:S(2)}) copy-start(f32[1,2,2,128]{3,1,2,0:T(2,128)} %copy-done.42) | copy-start | bytes 6148
  376.0 15.4 %copy-start.35 = (f32[512]{0:T(512)S(1)}, f32[512]{0:T(512)}, u32[]{:S(2)}) copy-start(f32[512]{0:T(512)} %copy-done.34) | copy-start | bytes 6148
  377.2 55.4 %copy-start.15 = (bf16[2,256,384]{2,1,0:T(8,128)(2,1)S(1)}, bf16[2,256,384]{2,1,0:T(8,128)(2,1)}, u32[]{:S(2)}) copy-start(bf16[2,256,384]{2,1,0:T(8,128)(2,1)} %param.29) | copy-start | bytes 1179652
  385.0 154.1 %copy-start.1 = (bf16[960,384]{1,0:T(8,128)(2,1)S(1)}, bf16[960,384]{1,0:T(8,128)(2,1)}, u32[]{:S(2)}) copy-start(bf16[960,384]{1,0:T(8,128)(2,1)} %param.24) | copy-start | bytes 2211844
Sparse Core Ops, SparseCore 0:
  332.4 20.9 reduce-scatter.1
  385.1 142.5 all-reduce.4

commit v2 on v1

--- a/solution.py
+++ b/solution.py
@@ -1,3 +1,5 @@
+import types
+
 import jax
 import jax.numpy as jnp
 from jax import lax
@@ -10,24 +12,6 @@
 
 EPS = 1e-06
 HIGH = lax.Precision.HIGHEST
-
-
-def normalize(value, gain, bias):
-    mean = jnp.mean(value, -1, keepdims=True)
-    centred = value - mean
-    spread = jnp.mean(centred * centred, -1, keepdims=True)
-    return centred * lax.rsqrt(spread + EPS) * gain + bias
-
-
-def gate_weights(logits, picks_hot):
-    chosen = jnp.sum(picks_hot * logits[..., None, :], -1)
-    return jax.nn.softmax(chosen, -1)
-
-
-def activate(value):
-    return jax.nn.gelu(value, approximate=True)
-
-
 F32 = jnp.float32
 LOW = jnp.bfloat16
 MESH = pl.DeviceIdType.MESH
@@ -40,6 +24,215 @@
 
 def dot_nt(a, b):
     return lax.dot_general(a, b, (((1,), (1,)), ((), ())), preferred_element_type=F32)
+
+
+def dot_tn(a, b):
+    return lax.dot_general(a, b, (((0,), (0,)), ((), ())), preferred_element_type=F32)
+
+
+def remote(src, dst, send, recv, device):
+    return pltpu.make_async_remote_copy(
+        src_ref=src, dst_ref=dst, send_sem=send, recv_sem=recv,
+        device_id=device, device_id_type=MESH,
+    )
+
+
+def run_kernel(kernel, name, ins, outs, scratch, collective):
+    names = [*ins, *outs, *scratch]
+
+    def body(*refs):
+        kernel(types.SimpleNamespace(**dict(zip(names, refs, strict=True))))
+
+    made = pl.pallas_call(
+        body,
+        name=name,
+        out_shape=[jax.ShapeDtypeStruct(shape, dtype) for shape, dtype, _ in outs.values()],
+        in_specs=[pl.BlockSpec(memory_space=space) for _, space in ins.values()],
+        out_specs=[pl.BlockSpec(memory_space=space) for _, _, space in outs.values()],
+        scratch_shapes=list(scratch.values()),
+        compiler_params=pltpu.CompilerParams(
+            collective_id=collective, has_side_effects=True, vmem_limit_bytes=62 * MIB
+        ),
+    )(*[array for array, _ in ins.values()])
+    return types.SimpleNamespace(**dict(zip(outs, made, strict=True)))
+
+
+def center(value):
+    mean = jnp.mean(value, -1, keepdims=True)
+    centred = value - mean
+    scale = lax.rsqrt(jnp.mean(centred * centred, -1, keepdims=True) + EPS)
+    return centred * scale, scale
+
+
+def center_back(grad, normal, scale, gain):
+    inner = grad * gain
+    mean = jnp.mean(inner, -1, keepdims=True)
+    along = jnp.mean(inner * normal, -1, keepdims=True)
+    return scale * (inner - mean - normal * along)
+
+
+def head_maps(heads, head):
+    row = lax.broadcasted_iota(jnp.int32, (heads * head, 2 * head), 0)
+    row = lax.rem(row, head)
+    col = lax.broadcasted_iota(jnp.int32, (heads * head, 2 * head), 1)
+    low = jnp.where(row == col, 1.0, 0.0).astype(LOW)
+    high = jnp.where(row + head == col, 1.0, 0.0).astype(LOW)
+    return low, high
+
+
+def masked_softmax(logits, chosen, axis):
+    top = jnp.max(jnp.where(chosen, logits, -1e30), axis, keepdims=True)
+    expo = jnp.where(chosen, jnp.exp(jnp.minimum(logits - top, 0.0)), 0.0)
+    return expo / jnp.sum(expo, axis, keepdims=True)
+
+
+def front_kernel(v):
+    dp = lax.axis_index("dp")
+    ex = lax.axis_index("expert")
+    count, d = v.tok.shape
+    half = count // 2
+    heads = v.qa.shape[1]
+    head = v.kv.shape[2] // 2
+    picks = v.pick.shape[1]
+
+    def peer(r):
+        return (dp ^ (r // 4), ex ^ (r % 4))
+
+    barrier = pltpu.get_barrier_semaphore()
+    for r in range(1, 8):
+        pl.semaphore_signal(barrier, 1, device_id=peer(r), device_id_type=MESH)
+
+    def cot_copy(r):
+        return remote(v.cot, v.ca.at[r], v.cs.at[r], v.cv.at[r], peer(r))
+
+    def cot_forward(r):
+        return remote(v.ca.at[r], v.ca.at[r + 1], v.cs.at[r + 1], v.cv.at[r + 1], peer(1))
+
+    def kv_copy(r):
+        return remote(
+            v.kv.at[:, pl.ds(0, half), :], v.kv.at[:, pl.ds(r * half, half), :],
+            v.ks.at[r], v.kr.at[r], peer(r),
+        )
+
+    gain = v.gain[...]
+    bias = v.bias[...]
+    for i in range(2):
+        rows = slice(i * half, (i + 1) * half)
+        normal, _ = center(v.tok[rows, :].astype(F32))
+        normed = (normal * gain[0:1] + bias[0:1]).astype(LOW)
+        v.n1[rows, :] = normed
+        v.kv[i, 0:half, :] = dot(normed, v.wkv[...]).astype(LOW)
+    pl.semaphore_wait(barrier, 7)
+    for r in (1, 2, 3):
+        kv_copy(r).start()
+    for r in (1, 2, 4, 6):
+        cot_copy(r).start()
+    v.qa[...] = dot(v.n1[...], v.wq[...]).astype(LOW)
+
+    experts = v.router1.shape[1]
+    number = lax.broadcasted_iota(jnp.int32, (experts, count), 0)
+    chosen = number == v.pickt[0:1, :]
+    for k in range(1, picks):
+        chosen = chosen | (number == v.pickt[k:k + 1, :])
+    earlier = lax.broadcasted_iota(jnp.int32, (count, count), 0) < lax.broadcasted_iota(
+        jnp.int32, (count, count), 1
+    )
+    before = dot(jnp.where(chosen, 1.0, 0.0).astype(LOW), jnp.where(earlier, 1.0, 0.0).astype(LOW))
+    rank = jnp.where(chosen, before, -1.0)
+
+    to_query, to_value = head_maps(heads // head, head)
+    owner = lax.broadcasted_iota(jnp.int32, (half, heads), 1)
+    owner = lax.div(owner, head)
+    lane = lax.broadcasted_iota(jnp.int32, (half, experts), 1)
+    wide = lax.broadcasted_iota(jnp.int32, (half, 2 * head), 1)
+    for r in (1, 2, 3):
+        kv_copy(r).wait_recv()
+
+    for i in range(2):
+        rows = slice(i * half, (i + 1) * half)
+        logits = dot_nt(v.n1[rows, :], v.router1[v.task[i]])
+        named = [lane == v.pick[rows, k:k + 1] for k in range(picks)]
+        allowed = named[0]
+        for k in range(1, picks):
+            allowed = allowed | named[k]
+        gates = masked_softmax(logits, allowed, 1)
+        v.g1[rows, :] = gates
+        kv = v.kv[i]
+        for k in range(picks):
+            mine = owner == v.pick[rows, k:k + 1]
+            gate = jnp.sum(jnp.where(named[k], gates, 0.0), 1, keepdims=True)
+            all_queries = v.qa[rows, :]
+            query = dot(jnp.where(mine, all_queries, jnp.zeros_like(all_queries)), to_query)
+            query = (query * head ** -0.5).astype(LOW)
+            v.q8[picks * i + k] = query
+            scores = dot_nt(query, kv)
+            expo = jnp.exp(scores - jnp.max(scores, 1, keepdims=True))
+            total = jnp.sum(expo, 1, keepdims=True)
+            low = expo.astype(LOW)
+            v.eb[picks * i + k] = low
+            attended = dot(low, kv) / total
+            v.att[picks * i + k] = jnp.where(wide == 0, total, attended)
+            spread = dot_nt((gate * attended).astype(LOW), to_value).astype(LOW)
+            if k == 0:
+                v.heads[rows, :] = jnp.where(mine, spread, jnp.zeros_like(spread))
+            else:
+                v.heads[rows, :] = jnp.where(mine, spread, v.heads[rows, :])
+        middle = v.tok[rows, :].astype(F32) + dot(v.heads[rows, :], v.wo[...])
+        v.mid[rows, :] = middle
+        normal, _ = center(middle)
+        normed = (normal * gain[1:2] + bias[1:2]).astype(LOW)
+        v.n2[rows, :] = normed
+        logits = dot_nt(v.router2[v.task[i]], normed)
+        gates = masked_softmax(logits, rank[:, rows] >= 0.0, 0)
+        v.g2[:, rows] = gates
+        for g in range(8):
+            v.meta[g, 0:2, rows] = rank[2 * g:2 * g + 2, rows]
+            v.meta[g, 2:4, rows] = gates[2 * g:2 * g + 2, :]
+            v.meta[g, 4:16, rows] = jnp.zeros((12, half), F32)
+        if i == 0:
+            for r in (2, 4, 6):
+                cot_copy(r).wait_recv()
+                cot_forward(r).start()
+
+    v.ca[0] = v.cot[...]
+    for r in (1, 3, 5, 7):
+        cot_copy(r).wait_recv()
+    for r in (1, 2, 3):
+        kv_copy(r).wait_send()
+    for r in (1, 2, 4, 6):
+        cot_copy(r).wait_send()
+    for r in (2, 4, 6):
+        cot_forward(r).wait_send()
+
+
+def front_call(tok, cot, pick, pickt, task, gain, bias, wq, wkv, wo, router1, router2):
+    count, d = tok.shape
+    heads = wq.shape[1]
+    width = wkv.shape[1]
+    picks = pick.shape[1]
+    half = count // 2
+    vm = pltpu.VMEM
+    dma = pltpu.SemaphoreType.DMA
+    return run_kernel(
+        front_kernel, "front",
+        dict(
+            tok=(tok, vm), cot=(cot, vm), pick=(pick, vm), pickt=(pickt, vm), task=(task, pltpu.SMEM),
+            gain=(gain, vm), bias=(bias, vm), wq=(wq, vm), wkv=(wkv, vm), wo=(wo, vm),
+            router1=(router1, vm), router2=(router2, vm),
+        ),
+        dict(
+            n1=((count, d), LOW, vm), n2=((count, d), LOW, vm), mid=((count, d), F32, vm),
+            ca=((8, count, d), LOW, vm), heads=((count, heads), LOW, vm),
+            kv=((2, 4 * half, width), LOW, vm), q8=((2 * picks, half, width), LOW, vm),
+            eb=((2 * picks, half, 4 * half), LOW, vm), att=((2 * picks, half, width), F32, vm),
+            g1=((count, 16), F32, vm), g2=((16, count), F32, vm), meta=((8, 16, count), F32, vm),
+        ),
+        dict(
+            qa=pltpu.VMEM((count, heads), LOW),
+            cs=dma((8,)), cv=dma((8,)), ks=dma((4,)), kr=dma((4,)),
+        ),
+        1,
+    )
 
 
 def gelu_parts(value):
@@ -52,10 +245,10 @@
 
 
 def expert_kernel(
-    x_ref, c_ref, m_ref, we_hbm, wr_hbm,
+    x_ref, ca, m_ref, we_hbm, wr_hbm,
     fin_ref, grn_ref, dg_ref, gout,
-    xa, ca, ma, we, wr, xr, gp, xrt, gpt, cr, act, gh, pr, gr, ra, rb, rt2, rc, rx, dgs,
-    wsem, xs, xv, cs, cv, ms, mv, gs, gv, s1s, s1r, s2s, s2r, s3s, ys, yr, ls, k1s, k1r, k2s, k2r,
+    xa, ma, we, wr, xr, gp, xrt, gpt, cr, act, gh, pr, gr, ra, rb, rt2, rc, rx, dgs,
+    wsem, xs, xv, ms, mv, gs, gv, s1s, s1r, s2s, s2r, s3s, ys, yr, ls, k1s, k1r, k2s, k2r,
 ):
     dp = lax.axis_index("dp")
     ex = lax.axis_index("expert")
@@ -75,12 +268,6 @@
     def group(r):
         return 2 * (ex ^ (r % 4)) + (y ^ (r // 4))
 
-    def remote(src, dst, send, recv, device):
-        return pltpu.make_async_remote_copy(
-            src_ref=src, dst_ref=dst, send_sem=send, recv_sem=recv,
-            device_id=device, device_id_type=MESH,
-        )
-
     barrier = pltpu.get_barrier_semaphore()
     for r in range(1, 8):
         pl.semaphore_signal(barrier, 1, device_id=peer(r), device_id_type=MESH)
@@ -97,27 +284,20 @@
     for load in loads:
         load.start()
     xa[0] = x_ref[...]
-    ca[0] = c_ref[...]
     ma[0] = m_ref[group(0)]
 
     pl.semaphore_wait(barrier, jnp.where(is_mid, 9, 8))
 
     def gather_copies(r):
         device = peer(r)
-        return (
-            remote(xa.at[0], xa.at[r], xs.at[r], xv.at[r], device),
-            remote(ca.at[0], ca.at[r], cs.at[r], cv.at[r], device),
-        )
+        return (remote(xa.at[0], xa.at[r], xs.at[r], xv.at[r], device),)
 
     def meta_copy(r):
         return remote(m_ref.at[group(r)], ma.at[r], ms.at[r], mv.at[r], peer(r))
 
     def forward_copies(r):
         device = peer(1)
-        return (
-            remote(xa.at[r], xa.at[r + 1], xs.at[r + 1], xv.at[r + 1], device),
-            remote(ca.at[r], ca.at[r + 1], cs.at[r + 1], cv.at[r + 1], device),
-        )
+        return (remote(xa.at[r], xa.at[r + 1], xs.at[r + 1], xv.at[r + 1], device),)
 
     direct = (1, 2, 4, 6)
     sent = [copy for r in direct for copy in gather_copies(r)]
@@ -374,7 +554,6 @@
         out_specs=(vmem, vmem, vmem, anywhere),
         scratch_shapes=[
             pltpu.VMEM((8, count, d), LOW),
-            pltpu.VMEM((8, count, d), LOW),
             pltpu.VMEM((8, 16, count), F32),
             pltpu.VMEM((2, d, ff), LOW),
             pltpu.VMEM((2, ff, d), LOW),
@@ -394,7 +573,7 @@
             pltpu.VMEM((4, CAP, ff), LOW),
             pltpu.VMEM((8, 2, 8, count), F32),
             dma((4,)),
-            dma((8,)), dma((8,)), dma((8,)), dma((8,)), dma((8,)), dma((8,)), dma((8,)), dma((8,)),
+            dma((8,)), dma((8,)), dma((8,)), dma((8,)), dma((8,)), dma((8,)),
             dma((chunks,)), dma((chunks,)), dma((chunks,)), dma((chunks,)), dma((chunks,)),
             dma((chunks,)), dma((chunks,)), dma((chunks,)),
             dma((4,)), dma((4,)), dma((4,)), dma((4,)),
@@ -431,10 +610,433 @@
     )(chunks, chunks)
 
 
-def masked_softmax(logits, chosen):
-    top = jnp.max(jnp.where(chosen > 0, logits, -jnp.inf), -1, keepdims=True)
-    expo = jnp.where(chosen > 0, jnp.exp(logits - top), 0.0)
-    return expo / jnp.sum(expo, -1, keepdims=True)
+ROWS_OUT, ROWS_TWO, ROWS_QUERY, ROWS_PAIR, ROWS_ONE = 0, 960, 1168, 2128, 2256
+PIECE = 320
+
+
+def back_first(v):
+    count, d = v.cot.shape
+    half = count // 2
+    experts = v.router2.shape[1]
+    grad_gates = jnp.concatenate([v.dg[g, j, 0:1, :] for g in range(8) for j in range(2)], 0)
+    gates = v.g2[...]
+    grad_logits = gates * (grad_gates - jnp.sum(gates * grad_gates, 0, keepdims=True))
+    grad_logits = grad_logits.astype(LOW)
+    gain = v.gain[1:2]
+    v.pay[...] = jnp.zeros_like(v.pay)
+    v.small[0] = jnp.zeros_like(v.small[0])
+    per_image = []
+    grad_gain = jnp.zeros((1, d), F32)
+    grad_bias = jnp.zeros((1, d), F32)
+    for i in range(2):
+        rows = slice(i * half, (i + 1) * half)
+        grad = v.grn[rows, :] + dot_tn(grad_logits[:, rows], v.router2[v.task[i]])
+        per_image.append(dot(grad_logits[:, rows], v.n2[rows, :]))
+        normal, scale = center(v.mid[rows, :])
+        grad_gain = grad_gain + jnp.sum(grad * normal, 0, keepdims=True)
+        grad_bias = grad_bias + jnp.sum(grad, 0, keepdims=True)
+        total = v.cot[rows, :].astype(F32) + center_back(grad, normal, scale, gain)
+        v.gmid[rows, :] = total
+        low = total.astype(LOW)
+        v.gbranch[rows, :] = low
+        v.gheads[rows, :] = dot_nt(low, v.wo[...]).astype(LOW)
+    v.small[0, 1:2, :] = grad_gain
+    v.small[0, 3:4, :] = grad_bias
+    v.pay[ROWS_OUT:ROWS_OUT + v.heads.shape[1], :] = dot_tn(v.heads[...], v.gbranch[...]).astype(LOW)
+    place_tasks(v, ROWS_TWO, per_image, experts)
+
+
+def place_tasks(v, start, per_image, experts):
+    for j in range(v.router1.shape[0]):
+        mine = [jnp.where(v.task[i] == j, per_image[i], 0.0) for i in range(2)]
+        at = start + j * experts
+        v.pay[at:at + experts, :] = (mine[0] + mine[1]).astype(LOW)
+
+
+def back_attention(v, i, dp, ex):
+    count, d = v.cot.shape
+    half = count // 2
+    heads = v.heads.shape[1]
+    head = v.kv.shape[2] // 2
+    picks = v.pick.shape[1]
+    experts = v.router1.shape[1]
+    to_query, to_value = head_maps(heads // head, head)
+    owner = lax.div(lax.broadcasted_iota(jnp.int32, (half, heads), 1), head)
+    lane = lax.broadcasted_iota(jnp.int32, (half, experts), 1)
+    rows = slice(i * half, (i + 1) * half)
+    kv = v.kv[i]
+    gates = v.g1[rows, :]
+    grad_gates = jnp.zeros((half, experts), F32)
+    grad_pair = jnp.zeros((2 * head, 4 * half), F32)
+    for k in range(picks):
+        at = picks * i + k
+        mine = owner == v.pick[rows, k:k + 1]
+        named = lane == v.pick[rows, k:k + 1]
+        gate = jnp.sum(jnp.where(named, gates, 0.0), 1, keepdims=True)
+        grad_heads = v.gheads[rows, :]
+        grad = dot(jnp.where(mine, grad_heads, jnp.zeros_like(grad_heads)), to_value)
+        attended = v.att[at]
+        total = attended[:, 0:1]
+        grad_gates = grad_gates + jnp.where(named, jnp.sum(grad * attended, 1, keepdims=True), 0.0)
+        grad = ((gate * grad).astype(LOW).astype(F32) / total).astype(LOW)
+        inner = jnp.sum(grad.astype(F32) * attended, 1, keepdims=True)
+        expo = v.eb[at]
+        grad_scores = (expo.astype(F32) * (dot_nt(grad, kv) - inner)).astype(LOW)
+        grad_query = (dot(grad_scores, kv) * head ** -0.5).astype(LOW)
+        spread = dot_nt(grad_query, to_query).astype(LOW)
+        if k == 0:
+            v.gqa[rows, :] = jnp.where(mine, spread, jnp.zeros_like(spread))
+        else:
+            v.gqa[rows, :] = jnp.where(mine, spread, v.gqa[rows, :])
+        grad_pair = grad_pair + dot(v.q8[at].astype(F32).T.astype(LOW), grad_scores)
+        grad_pair = grad_pair + dot(grad.astype(F32).T.astype(LOW), expo)
+    grad_logits = gates * (grad_gates - jnp.sum(gates * grad_gates, 1, keepdims=True))
+    v.gl1[rows, :] = grad_logits.astype(LOW)
+    for r in range(4):
+        v.dkv[r, i] = grad_pair[:, r * half:(r + 1) * half].astype(LOW)
+
+
+def pair_copy(v, r, dp, ex):
+    return remote(v.dkv.at[r], v.din.at[r], v.ps.at[r], v.pr.at[r], (dp, ex ^ r))
+
+
+def back_last(v):
+    count, d = v.cot.shape
+    half = count // 2
+    experts = v.router1.shape[1]
+    heads = v.heads.shape[1]
+    width = v.kv.shape[2]
+    gain = v.gain[0:1]
+    grad_gain = jnp.zeros((1, d), F32)
+    grad_bias = jnp.zeros((1, d), F32)
+    grad_pair = jnp.zeros((width, d), F32)
+    per_image = []
+    for i in range(2):
+        rows = slice(i * half, (i + 1) * half)
+        pair = v.dkv[0, i].astype(F32)
+        for r in (1, 2, 3):
+            pair = pair + v.din[r, i].astype(F32)
+        grad_pair = grad_pair + dot(pair.astype(LOW), v.n1[rows, :])
+        grad = dot_nt(v.gqa[rows, :], v.wq[...]) + dot_nt(pair.T.astype(LOW), v.wkv[...])
+        grad = grad + dot(v.gl1[rows, :], v.router1[v.task[i]])
+        per_image.append(dot_tn(v.gl1[rows, :], v.n1[rows, :]))
+        normal, scale = center(v.tok[rows, :].astype(F32))
+        grad_gain = grad_gain + jnp.sum(grad * normal, 0, keepdims=True)
+        grad_bias = grad_bias + jnp.sum(grad, 0, keepdims=True)
+        v.gtok[rows, :] = v.gmid[rows, :] + center_back(grad, normal, scale, gain)
+    v.small[0, 0:1, :] = grad_gain
+    v.small[0, 2:3, :] = grad_bias
+    v.pay[ROWS_QUERY:ROWS_QUERY + heads, :] = dot_tn(v.gqa[...], v.n1[...]).astype(LOW)
+    v.pay[ROWS_PAIR:ROWS_PAIR + width, :] = grad_pair.astype(LOW)
+    place_tasks(v, ROWS_ONE, per_image, experts)
+
+
+def count_usage(v):
+    count, d = v.cot.shape
+    half = count // 2
+    experts = v.router1.shape[1]
+    picks = v.pick.shape[1]
+    lane = lax.broadcasted_iota(jnp.int32, (half, d), 1)
+    task = lax.broadcasted_iota(jnp.int32, (experts, d), 0)
+    for which, ref in enumerate((v.pick, v.pick2)):
+        table = jnp.zeros((experts, d), F32)
+        for i in range(2):
+            rows = slice(i * half, (i + 1) * half)
+            named = jnp.zeros((half, d), F32)
+            for k in range(picks):
+                named = named + jnp.where(lane == ref[rows, k:k + 1], 1.0, 0.0)
+            table = table + jnp.where(task == v.task[i], jnp.sum(named, 0, keepdims=True), 0.0)
+        v.small[0, 8 + which * experts:8 + (which + 1) * experts, :] = table
+
+
+def shared_reduce(v, dp, ex, pause):
+    y = lax.rem(dp, 2)
+    z = lax.div(dp, 2)
+    is_end = (z == 0) | (z == 3)
+    is_mid = (z == 1) | (z == 2)
+    toward = jnp.where(z < 2, dp + 2, dp - 2)
+    outer = jnp.where(z == 1, dp - 2, jnp.where(z == 2, dp + 2, dp))
+    core = lax.rem(ex, 2)
+    mine = y * 2 + lax.div(ex, 2)
+    side = 4 * PIECE
+
+    def part(ref, c, q):
+        return ref.at[pl.ds(pl.multiple_of(c * side + q * PIECE, PIECE), PIECE), :]
+
+    def whole(ref, c):
+        return ref.at[pl.ds(pl.multiple_of(c * side, side), side), :]
+
+    def exchange(stage, device):
+        return remote(v.small.at[stage], v.small_in.at[stage], v.ss.at[stage], v.sr.at[stage], device)
+
+    def plane(r):
+        return (dp ^ (r // 2), ex ^ (2 * (r % 2)))
+
+    partner = (dp, ex ^ 1)
+    first = remote(whole(v.pay, 1 - core), v.half_in, v.as_.at[0], v.ar.at[0], partner)
+    first.start()
+    small = exchange(0, partner)
+    small.start()
+    small.wait_recv()
+    v.small[1] = v.small[0] + v.small_in[0]
+    small1 = exchange(1, plane(1))
+    small1.start()
+    first.wait_recv()
+    own = whole(v.pay, core)
+    own[...] = (own[...].astype(F32) + v.half_in[...].astype(F32)).astype(LOW)
+    scatter = [
+        remote(part(v.pay, core, mine ^ r), v.piece_in.at[r], v.as_.at[r], v.ar.at[r], plane(r))
+        for r in (1, 2, 3)
+    ]
+    for copy in scatter:
+        copy.start()
+    small1.wait_recv()
+    v.small[2] = v.small[1] + v.small_in[1]
+    small2 = exchange(2, plane(2))
+    small2.start()
+    pause(0)
+    small2.wait_recv()
+    v.small[3] = v.small[2] + v.small_in[2]
+    for copy in scatter:
+        copy.wait_recv()
+    own = part(v.pay, core, mine)
+    total = own[...].astype(F32)
+    for r in (1, 2, 3):
+        total = total + v.piece_in[r].astype(F32)
+    own[...] = total.astype(LOW)
+
+    in_end = remote(own, v.zb, v.zs.at[0], v.zr.at[0], (toward, ex))
+    in_small = remote(v.small.at[3], v.small_in.at[3], v.zs.at[1], v.zr.at[1], (toward, ex))
+    mid = remote(v.zb, v.zc, v.zs.at[0], v.zr.at[2], (toward, ex))
+    mid_small = remote(v.small.at[4], v.small_in.at[4], v.zs.at[1], v.zr.at[3], (toward, ex))
+    spread = part(v.shared, core, mine)
+    out_mid = remote(spread, spread, v.zs.at[2], v.zr.at[4], (outer, ex))
+    out_small = remote(v.stats, v.stats, v.zs.at[3], v.zr.at[5], (outer, ex))
+
+    @pl.when(is_end)
+    def _():
+        in_end.start()
+        in_small.start()
+
+    pause(1)
+
+    @pl.when(is_mid)
+    def _():
+        in_end.wait_recv()
+        v.zb[...] = (own[...].astype(F32) + v.zb[...].astype(F32)).astype(LOW)
+        mid.start()
+        in_small.wait_recv()
+        v.small[4] = v.small[3] + v.small_in[3]
+        mid_small.start()
+
+    pause(2)
+
+    @pl.when(is_mid)
+    def _():
+        mid.wait_recv()
+        spread[...] = (v.zb[...].astype(F32) + v.zc[...].astype(F32)).astype(LOW)
+        out_mid.start()
+        mid_small.wait_recv()
+        v.stats[...] = v.small[4] + v.small_in[4]
+        out_small.start()
+
+    pause(3)
+
+    @pl.when(is_end)
+    def _():
+        out_mid.wait_recv()
+        out_small.wait_recv()
+
+    gather = [remote(spread, spread, v.bs.at[r], v.br.at[r], plane(r)) for r in (1, 2, 3)]
+    for copy in gather:
+        copy.start()
+    pause(4)
+    for r in (1, 2, 3):
+        there = part(v.shared, core, mine ^ r)
+        remote(there, there, v.bs.at[r], v.br.at[r], plane(r)).wait_recv()
+    last = remote(whole(v.shared, core), whole(v.shared, core), v.bs.at[0], v.br.at[0], partner)
+    last.start()
+    other = whole(v.shared, 1 - core)
+    remote(other, other, v.bs.at[0], v.br.at[0], partner).wait_recv()
+
+    first.wait_send()
+    for copy in [small, small1, small2, *scatter, *gather, last]:
+        copy.wait_send()
+
+    @pl.when(is_end)
+    def _():
+        in_end.wait_send()
+        in_small.wait_send()
+
+    @pl.when(is_mid)
+    def _():
+        mid.wait_send()
+        mid_small.wait_send()
+        out_mid.wait_send()
+        out_small.wait_send()
+
+
+def back_kernel(v):
+    dp = lax.axis_index("dp")
+    ex = lax.axis_index("expert")
+    z = lax.div(dp, 2)
+    is_mid = (z == 1) | (z == 2)
+    toward = jnp.where(z < 2, dp + 2, dp - 2)
+    outer = jnp.where(z == 1, dp - 2, jnp.where(z == 2, dp + 2, dp))
+    barrier = pltpu.get_barrier_semaphore()
+    for r in range(1, 8):
+        pl.semaphore_signal(
+            barrier, 1, device_id=(dp ^ (r // 4), ex ^ (r % 4)), device_id_type=MESH
+        )
+    pl.semaphore_signal(barrier, 1, device_id=(toward, ex), device_id_type=MESH)
+
+    @pl.when(is_mid)
+    def _():
+        pl.semaphore_signal(barrier, 1, device_id=(outer, ex), device_id_type=MESH)
+
+    v.out[...] = (v.mid[...] + v.fin[...]).astype(LOW)
+    back_first(v)
+    count_usage(v)
+    pl.semaphore_wait(barrier, jnp.where(is_mid, 9, 8))
+    for i in range(2):
+        back_attention(v, i, dp, ex)
+    for r in (1, 2, 3):
+        pair_copy(v, r, dp, ex).start()
+    for r in (1, 2, 3):
+        pair_copy(v, r, dp, ex).wait_recv()
+    back_last(v)
+    shared_reduce(v, dp, ex, lambda stage: None)
+    for r in (1, 2, 3):
+        pair_copy(v, r, dp, ex).wait_send()
+
+
+def back_scratch(count, d, heads, width):
+    half = count // 2
+    dma = pltpu.SemaphoreType.DMA
+    return dict(
+        pay=pltpu.VMEM((8 * PIECE, d), LOW),
+        small=pltpu.VMEM((5, 40, d), F32), small_in=pltpu.VMEM((5, 40, d), F32),
+        gmid=pltpu.VMEM((count, d), F32), gbranch=pltpu.VMEM((count, d), LOW),
+        gheads=pltpu.VMEM((count, heads), LOW), gqa=pltpu.VMEM((count, heads), LOW),
+        gl1=pltpu.VMEM((count, 16), LOW),
+        dkv=pltpu.VMEM((4, 2, width, half), LOW), din=pltpu.VMEM((4, 2, width, half), LOW),
+        half_in=pltpu.VMEM((4 * PIECE, d), LOW), piece_in=pltpu.VMEM((4, PIECE, d), LOW),
+        zb=pltpu.VMEM((PIECE, d), LOW), zc=pltpu.VMEM((PIECE, d), LOW),
+        ps=dma((4,)), pr=dma((4,)), ss=dma((4,)), sr=dma((4,)), as_=dma((4,)), ar=dma((4,)),
+        zs=dma((4,)), zr=dma((6,)), bs=dma((4,)), br=dma((4,)),
+    )
+
+
+def back_call(f, tok, cot, pick, pick2, task, gain, wq, wkv, wo, router1, router2, fin, grn, dg):
+    count, d = tok.shape
+    vm = pltpu.VMEM
+    return run_kernel(
+        back_kernel, "back",
+        dict(
+            tok=(tok, vm), cot=(cot, vm), pick=(pick, vm), pick2=(pick2, vm), task=(task, pltpu.SMEM),
+            gain=(gain, vm), wq=(wq, vm), wkv=(wkv, vm), wo=(wo, vm),
+            router1=(router1, vm), router2=(router2, vm),
+            n1=(f.n1, vm), n2=(f.n2, vm), mid=(f.mid, vm), heads=(f.heads, vm), kv=(f.kv, vm),
+            q8=(f.q8, vm), eb=(f.eb, vm), att=(f.att, vm), g1=(f.g1, vm), g2=(f.g2, vm),
+            fin=(fin, vm), grn=(grn, vm), dg=(dg, vm),
+        ),
+        dict(
+            out=((count, d), LOW, vm), gtok=((count, d), F32, vm),
+            shared=((8 * PIECE, d), LOW, vm), stats=((40, d), F32, vm),
+        ),
+        back_scratch(count, d, wq.shape[1], wkv.shape[1]),
+        2,
+    )
+
+
+def body_fast(
+    tokens,
+    task_ids,
+    attention_picks,
+    feedforward_picks,
+    norm_gain,
+    norm_bias,
+    query_weight,
+    key_weight,
+    value_weight,
+    output_weight,
+    attention_router,
+    feedforward_router,
+    expand_weight,
+    reduce_weight,
+    cotangent,
+):
+    images, patches, width = tokens.shape
+    count = images * patches
+    tasks, _, experts = attention_router.shape
+    head = key_weight.shape[1]
+    picks = attention_picks.shape[2]
+    slots = expand_weight.shape[0]
+    ff = expand_weight.shape[2]
+    wide = query_weight.shape[1]
+    tok = tokens.reshape(count, width)
+    cot = cotangent.reshape(count, width)
+    pick = attention_picks.reshape(count, picks)
+    pick2 = feedforward_picks.reshape(count, picks)
+    wkv = jnp.concatenate([key_weight, value_weight], 1)
+
+    def experts_first(router):
+        return jnp.pad(jnp.swapaxes(router, 1, 2), ((0, 0), (0, 16 - experts), (0, 0)))
+
+    router1 = experts_first(attention_router)
+    router2 = experts_first(feedforward_router)
+    f = front_call(
+        tok, cot, pick, pick2.T, task_ids, norm_gain, norm_bias, query_weight, wkv, output_weight,
+        router1, router2,
+    )
+    fin, grn, dg, chunks = experts_call(f.n2, f.ca, f.meta, expand_weight, reduce_weight)
+    b = back_call(
+        f, tok, cot, pick, pick2, task_ids, norm_gain, query_weight, wkv, output_weight,
+        router1, router2, fin, grn, dg,
+    )
+    grad_reduce, grad_expand = widen_call(chunks, slots, width, ff)
+
+    def section(start, rows):
+        return b.shared[start:start + rows].astype(F32)
+
+    def experts_last(start):
+        table = section(start, tasks * 16).reshape(tasks, 16, width)[:, :experts]
+        return jnp.swapaxes(table, 1, 2)
+
+    pair = section(ROWS_PAIR, 2 * head)
+    usage = b.stats[8:40, :experts].reshape(2, 16, experts)[:, :tasks]
+    return (
+        b.out.reshape(images, patches, width),
+        b.gtok.reshape(images, patches, width),
+        b.stats[0:2],
+        b.stats[2],
+        b.stats[3],
+        section(ROWS_QUERY, wide).T,
+        pair[:head].T,
+        pair[head:].T,
+        section(ROWS_OUT, wide),
+        experts_last(ROWS_ONE),
+        experts_last(ROWS_TWO),
+        grad_expand,
+        grad_reduce,
+        usage,
+    )
+
+
+def normalize(value, gain, bias):
+    mean = jnp.mean(value, -1, keepdims=True)
+    centred = value - mean
+    spread = jnp.mean(centred * centred, -1, keepdims=True)
+    return centred * lax.rsqrt(spread + EPS) * gain + bias
+
+
+def gate_weights(logits, picks_hot):
+    chosen = jnp.sum(picks_hot * logits[..., None, :], -1)
+    return jax.nn.softmax(chosen, -1)
+
+
+def activate(value):
+    return jax.nn.gelu(value, approximate=True)
 
 
 def body(
@@ -680,216 +1282,6 @@
     )
 
 
-def body_fast(
-    tokens,
-    task_ids,
-    attention_picks,
-    feedforward_picks,
-    norm_gain,
-    norm_bias,
-    query_weight,
-    key_weight,
-    value_weight,
-    output_weight,
-    attention_router,
-    feedforward_router,
-    expand_weight,
-    reduce_weight,
-    cotangent,
-):
-    images, patches, width = tokens.shape
-    count = images * patches
-    tasks = attention_router.shape[0]
-    experts = attention_router.shape[2]
-    head = key_weight.shape[1]
-    picks = attention_picks.shape[2]
-    slots = expand_weight.shape[0]
-    groups = lax.axis_size("expert")
-    lanes = groups * slots
-    f32 = jnp.float32
-    low_type = jnp.bfloat16
-    inputs = tokens.astype(f32).reshape(count, width)
-    expert_range = jnp.arange(experts, dtype=jnp.int32)
-    task_hot = (task_ids[:, None] == jnp.arange(tasks, dtype=jnp.int32)[None, :]).astype(f32)
-    task_low = task_hot.astype(low_type)
-    attend_hot = (attention_picks[..., None] == expert_range).astype(f32)
-    attend_low = attend_hot.astype(low_type)
-    choices = feedforward_picks.reshape(count, picks)
-    wide = jnp.arange(experts + 1, dtype=jnp.int32)
-    feed_hot = (choices[..., None] == expert_range).astype(f32)
-    chosen = jnp.sum((choices[..., None] == wide).astype(f32), 1)
-    earlier = jnp.arange(count)[:, None] > jnp.arange(count)[None, :]
-    before = jnp.dot(earlier.astype(low_type), chosen.astype(low_type), preferred_element_type=f32)
-    rank = jnp.where(chosen > 0, before, -1.0).T
-    first, first_back = jax.vjp(normalize, inputs, norm_gain[0], norm_bias[0])
-    normed_one = first.astype(low_type)
-    shaped_one = normed_one.reshape(images, patches, width)
-    router_one = jnp.einsum(
-        "it,tde->ide", task_low, attention_router, preferred_element_type=f32
-    ).astype(low_type)
-    logits_one = jnp.einsum("ipd,ide->ipe", shaped_one, router_one, preferred_element_type=f32)
-    gates_one, gates_one_back = jax.vjp(lambda value: gate_weights(value, attend_hot), logits_one)
-    queries_all = jnp.dot(normed_one, query_weight, preferred_element_type=f32).astype(low_type)
-    queries_all = queries_all.reshape(images, patches, experts, head)
-    queries = jnp.einsum(
-        "ipke,ipeh->ipkh", attend_low, queries_all, preferred_element_type=f32
-    ).astype(low_type)
-    queries = queries.reshape(images, patches * picks, head)
-    key_value = jnp.concatenate([key_weight, value_weight], 1)
-    pair = jnp.dot(normed_one, key_value, preferred_element_type=f32).astype(low_type)
-    pair = pair.reshape(images, patches, 2 * head)
-    pair_all = lax.all_gather(pair, "expert", axis=1, tiled=True)
-    keys_all = pair_all[:, :, :head]
-    values_all = pair_all[:, :, head:]
-    scores = jnp.einsum("irh,ish->irs", queries, keys_all, preferred_element_type=f32) * 0.125
-    top = jnp.max(scores, -1, keepdims=True)
-    expo = jnp.exp(scores - top)
-    total = jnp.sum(expo, -1, keepdims=True)
-    log_total = top + jnp.log(total)
-    probs_low = (expo / total).astype(low_type)
-    attended = jnp.einsum("irs,ish->irh", probs_low, values_all, preferred_element_type=f32)
-    attended = attended.reshape(images, patches, picks, head)
-    weighted = gates_one[..., None] * attended
-    heads = jnp.einsum("ipke,ipkh->ipeh", attend_hot, weighted, precision=HIGH)
-    heads = heads.reshape(count, experts * head).astype(low_type)
-    middle = inputs + jnp.dot(heads, output_weight, preferred_element_type=f32)
-    second, second_back = jax.vjp(normalize, middle, norm_gain[1], norm_bias[1])
-    normed_two = second.astype(low_type)
-    shaped_two = normed_two.reshape(images, patches, width)
-    router_two = jnp.einsum(
-        "it,tde->ide", task_low, feedforward_router, preferred_element_type=f32
-    ).astype(low_type)
-    logits_two = jnp.einsum(
-        "ipd,ide->ipe", shaped_two, router_two, preferred_element_type=f32
-    ).reshape(count, experts)
-    gates_two = masked_softmax(logits_two, chosen[:, :experts])
-    gate_rows = jnp.pad(gates_two, ((0, 0), (0, 1))).T
-    pairs = lanes // 2
-    meta = jnp.concatenate(
-        [
-            rank.reshape(pairs, 2, count),
-            gate_rows.reshape(pairs, 2, count),
-            jnp.zeros((pairs, 12, count), f32),
-        ],
-        1,
-    )
-    final_part, grad_normed_two, grad_gate_rows, grad_chunks = experts_call(
-        normed_two, cotangent.reshape(count, width), meta, expand_weight, reduce_weight
-    )
-    output = (middle + final_part).astype(low_type).reshape(images, patches, width)
-    grad_final = cotangent.astype(f32).reshape(count, width)
-    grad_gates = grad_gate_rows[:, :, 0].reshape(2 * pairs, count)[:experts].T
-    grad_logits_two = gates_two * (
-        grad_gates - jnp.sum(gates_two * grad_gates, -1, keepdims=True)
-    )
-    grad_logits_two = grad_logits_two.astype(low_type).reshape(images, patches, experts)
-    per_image_two = jnp.einsum(
-        "ipd,ipe->ide", shaped_two, grad_logits_two, preferred_element_type=f32
-    )
-    grad_feed_router = jnp.einsum("it,ide->tde", task_hot, per_image_two, precision=HIGH)
-    grad_normed_two = grad_normed_two + jnp.einsum(
-        "ipe,ide->ipd", grad_logits_two, router_two, preferred_element_type=f32
-    ).reshape(count, width)
-    grad_middle_norm, grad_gain_two, grad_bias_two = second_back(grad_normed_two)
-    grad_middle = grad_final + grad_middle_norm
-    grad_branch = grad_middle.astype(low_type)
-    grad_output = jnp.einsum("tc,td->cd", heads, grad_branch, preferred_element_type=f32)
-    grad_heads = jnp.einsum(
-        "td,cd->tc", grad_branch, output_weight, preferred_element_type=f32
-    ).astype(low_type)
-    grad_heads = grad_heads.reshape(images, patches, experts, head)
-    grad_selected = jnp.einsum(
-        "ipke,ipeh->ipkh", attend_low, grad_heads, preferred_element_type=f32
-    )
-    grad_gates_one = jnp.sum(attended * grad_selected, -1)
-    grad_attended = (
-        (gates_one[..., None] * grad_selected)
-        .astype(low_type)
-        .reshape(images, patches * picks, head)
-    )
-    scores_back = jnp.einsum("irh,ish->irs", queries, keys_all, preferred_element_type=f32) * 0.125
-    probs_back = jnp.exp(scores_back - log_total)
-    grad_values = jnp.einsum(
-        "irs,irh->ish", probs_back.astype(low_type), grad_attended, preferred_element_type=f32
-    )
-    grad_probs = jnp.einsum("irh,ish->irs", grad_attended, values_all, preferred_element_type=f32)
-    inner_sum = jnp.sum(probs_back * grad_probs, -1, keepdims=True)
-    grad_scores = (probs_back * (grad_probs - inner_sum)).astype(low_type)
-    grad_query_sel = (
-        jnp.einsum("irs,ish->irh", grad_scores, keys_all, preferred_element_type=f32) * 0.125
-    )
-    grad_keys = jnp.einsum("irs,irh->ish", grad_scores, queries, preferred_element_type=f32) * 0.125
-    grad_pair = jnp.concatenate([grad_keys, grad_values], -1)
-    pair_sum = lax.psum_scatter(
-        grad_pair.astype(jnp.bfloat16), "expert", scatter_dimension=1, tiled=True
-    ).astype(jnp.float32)
-    pair_sum = pair_sum.astype(low_type).reshape(count, 2 * head)
-    grad_query_sel = grad_query_sel.reshape(images, patches, picks, head)
-    grad_queries_all = jnp.einsum("ipke,ipkh->ipeh", attend_hot, grad_query_sel, precision=HIGH)
-    grad_queries_all = grad_queries_all.astype(low_type).reshape(count, experts * head)
-    grad_logits_one = gates_one_back(grad_gates_one)[0].astype(low_type)
-    per_image_one = jnp.einsum(
-        "ipd,ipe->ide", shaped_one, grad_logits_one, preferred_element_type=f32
-    )
-    grad_attend_router = jnp.einsum("it,ide->tde", task_hot, per_image_one, precision=HIGH)
-    grad_query = jnp.einsum("td,tc->dc", normed_one, grad_queries_all, preferred_element_type=f32)
-    grad_key_value = jnp.einsum("td,tc->dc", normed_one, pair_sum, preferred_element_type=f32)
-    grad_normed_one = jnp.einsum(
-        "tc,dc->td", grad_queries_all, query_weight, preferred_element_type=f32
-    )
-    grad_normed_one = grad_normed_one + jnp.einsum(
-        "tc,dc->td", pair_sum, key_value, preferred_element_type=f32
-    )
-    grad_normed_one = grad_normed_one + jnp.einsum(
-        "ipe,ide->ipd", grad_logits_one, router_one, preferred_element_type=f32
-    ).reshape(count, width)
-    grad_inputs_norm, grad_gain_one, grad_bias_one = first_back(grad_normed_one)
-    grad_tokens = (grad_middle + grad_inputs_norm).reshape(images, patches, width)
-    grad_gain = jnp.stack([grad_gain_one, grad_gain_two])
-    grad_bias = jnp.stack([grad_bias_one, grad_bias_two])
-    feed_shaped = feed_hot.reshape(images, patches, picks, experts)
-    usage = jnp.stack(
-        [
-            jnp.einsum("it,ipke->te", task_hot, attend_hot, precision=HIGH),
-            jnp.einsum("it,ipke->te", task_hot, feed_shaped, precision=HIGH),
-        ]
-    )
-    shared = lax.psum(
-        (
-            grad_query,
-            grad_key_value,
-            grad_output,
-            grad_attend_router,
-            grad_feed_router,
-            grad_gain,
-            grad_bias,
-            usage,
-        ),
-        ("dp", "expert"),
-    )
-    grad_reduce_sum, grad_expand_sum = widen_call(
-        grad_chunks, slots, width, expand_weight.shape[2]
-    )
-    grad_key_sum = shared[1][:, :head]
-    grad_value_sum = shared[1][:, head:]
-    return (
-        output,
-        grad_tokens,
-        shared[5],
-        shared[6][0],
-        shared[6][1],
-        shared[0],
-        grad_key_sum,
-        grad_value_sum,
-        shared[2],
-        shared[3],
-        shared[4],
-        grad_expand_sum,
-        grad_reduce_sum,
-        shared[7],
-    )
-
-
 def solution(mesh):
     placed = (
         P("dp", "expert", None),

time: 553 us -> 370 us (0.67)
  waiting for transfers between devices: 93.8 us -> 0 us
  Pallas kernels: 254 us -> 346 us
  matrix products: 59.1 us -> 0 us
  blocking collectives: 48.2 us -> 0 us
  other arithmetic: 34.1 us -> 4.32 us
  local copies, waits for them, and re-layouts: 42.1 us -> 16.8 us
  between operations: 15.2 us -> 0.74 us
    pallas_call x0 -> x2, Pallas kernels: none -> 110 us  [run_kernel(): pl.pallas_call(body, name=name, out_shape=[jax.ShapeDtypeStruct(shape, dt...]
    psum x1 -> x0, waiting for transfers between devices: 93.8 us -> none  [body_fast(): lax.psum((grad_query, grad_key_value, grad_output, grad_attend_router, gr...]
    dot_general x32 -> x0, matrix products: 59.1 us -> none  [the longest x1 6.43 us: body_fast(): jnp.einsum('ipke,ipkh->ipeh', attend_hot, grad_query_sel, precision=HIGH)]
    psum x1 -> x0, blocking collectives: 39.5 us -> none  [body_fast(): lax.psum((grad_query, grad_key_value, grad_output, grad_attend_router, gr...]
    reduce_sum x14 -> x0, other arithmetic: 22.4 us -> none  [the longest x1 7.35 us: gate_weights(): chosen = jnp.sum(picks_hot * logits[..., None, :], -1)]
    pallas_call x1, Pallas kernels: 235 us -> 217 us  [experts_call(): pl.pallas_call(expert_kernel, name='experts', out_shape=(jax.ShapeDtypeSt...]
    reshape x13 -> x0, local copies, waits for them, and re-layouts: 13.4 us -> none  [the longest x2 5.71 us: body_fast(): grad_heads = grad_heads.reshape(images, patches, experts, head)]
    unnamed x124 -> x18, local copies, waits for them, and re-layouts: 18.8 us -> 7.71 us
  transfers between devices with their start and end apart: 2 -> 0, of which waited for: 1 -> 0; matrix products, arithmetic and copies ran while one was open for 8% -> 0% of each run, Pallas kernels for 3% -> 0%
where the time goes in v2:
time: 370 us; the launch traced here: 368 us
  Pallas kernels  346 us (94%)
  local copies, waits for them, and re-layouts  16.8 us (5%)
  other arithmetic  4.32 us (1%)
    pallas_call x1, Pallas kernels, experts_call(): pl.pallas_call(expert_kernel, name='experts', out_shape=(jax.ShapeDtypeSt...  217 us
    pallas_call x2, Pallas kernels, run_kernel(): pl.pallas_call(body, name=name, out_shape=[jax.ShapeDtypeStruct(shape, dt...  110 us
    pallas_call x1, Pallas kernels, widen_call(): pl.pallas_call(widen_kernel, name='widen', grid=(slots, n), in_specs=[pl....  18.8 us
    unnamed x18, local copies, waits for them, and re-layouts  7.71 us

profile of v2, /device:TPU:0, one launch (start us, length us, event | category | flops | bytes accessed | tf_op | source)
XLA Modules:
  0.0 368.1 jit_solution(17965130510612509111)
XLA Ops:
  0.6 0.0 copy-start.3
  0.7 1.0 copy.31
  1.6 0.9 copy.32
  2.6 0.7 pad_maximum_fusion.refs_8_.refs_7_
  3.3 1.6 pad.7.refs_10_.refs_9_
  4.9 1.6 pad.8.refs_11_.refs_10_
  6.5 0.8 copy.30
  7.3 0.0 copy-start
  7.4 0.7 copy.33.refs_3_
  8.1 1.5 copy.29
  9.6 0.0 copy-done.3
  9.6 1.2 copy.35.refs_7_.refs_6_
  10.8 39.6 %front.1 = (bf16[512,384]{1,0:T(8,128)(2,1)}, bf16[512,384]{1,0:T(8,128)(2,1)}, f32[512,384]{1,0:T(8,128)}, bf16[8,512,384]{2,1,0:T(8,128)(2,1)}, bf16[512,960]{...) custom-call(bf16[512,384]{1,0:T(8,128)(2,1)} %bitcast.28, ...), custom_call_target="tpu_custom_call" | custom-call | tf_op jit(solution)/shard_map/front/pallas_call | solution.py:46
  50.4 0.0 copy-done
  50.4 217.1 %experts.1 = (f32[512,384]{1,0:T(8,128)}, f32[512,384]{1,0:T(8,128)}, f32[8,2,8,512]{3,2,1,0:T(8,128)}, bf16[48,384,256]{2,1,0:T(8,128)(2,1)}) custom-call(bf16[512,384]{1,0:T(8,128)(2,1)} %get-tuple-element.37.x_ref.refs_12_, bf16[8,512,384]{2,1,0:T(8,128)(2,1)} %get-tuple-element.46.ca, f32[8,16,512]{2,1,0:T(8,128)} %get-tuple-element.47.m_ref, ...), custom_call_target="tpu_custom_call" | custom-call | tf_op jit(solution)/shard_map/experts/pallas_call | solution.py:544
  267.4 70.8 %back.1 = (bf16[512,384]{1,0:T(8,128)(2,1)}, f32[512,384]{1,0:T(8,128)}, bf16[2560,384]{1,0:T(8,128)(2,1)}, f32[40,384]{1,0:T(8,128)}) custom-call(bf16[512,384]{1,0:T(8,128)(2,1)} %bitcast.29, bf16[512,384]{1,0:T(8,128)(2,1)} %bitcast.31, s32[512,4]{1,0:T(8,128)} %bitcast.25, s32[512,4]{1,0:T(8,128)} %bitcast.27, s32[2]{0:T(128)} %refs_4_.3, ...), custom_call_target="tpu_custom_call" | custom-call | tf_op jit(solution)/shard_map/back/pallas_call | solution.py:46
  338.3 0.0 copy-start.1
  338.3 1.4 slice.44
  339.7 1.4 slice_reduce_fusion
  341.1 0.7 slice.56
  341.8 0.6 copy.37
  342.4 0.9 slice_convert_fusion.1
  343.4 0.7 slice_bitcast_fusion
  344.0 1.0 fusion
  345.1 0.9 convert_bitcast_fusion.1
  346.0 0.0 copy-done.1
  346.0 1.8 slice_convert_fusion
  347.7 0.0 copy-start.4
  347.7 0.0 copy-start.2
  347.7 18.8 %widen.1 = (f32[4,1536,384]{2,1,0:T(8,128)}, f32[4,384,1536]{2,1,0:T(8,128)}) custom-call(bf16[48,384,256]{2,1,0:T(8,128)(2,1)} %get-tuple-element.55.r_ref.e_ref, bf16[48,384,256]{2,1,0:T(8,128)(2,1)} %get-tuple-element.55.r_ref.e_ref), custom_call_target="tpu_custom_call" | custom-call | tf_op jit(solution)/shard_map/widen/pallas_call | solution.py:594
  366.5 0.0 copy-done.4
  366.5 0.7 copy.40
  367.3 0.0 copy-done.2
  367.3 0.9 copy.41
Async XLA Ops:
  0.6 9.0 %copy-start.3 = (bf16[384,960]{0,1:T(8,128)(2,1)S(1)}, bf16[384,960]{0,1:T(8,128)(2,1)}, u32[]{:S(2)}) copy-start(bf16[384,960]{0,1:T(8,128)(2,1)} %param.21) | copy-start | bytes 2211844
  7.3 43.0 %copy-start = (s32[1,1,512,4]{3,2,1,0:T(8,128)}, s32[1,1,512,4]{3,2,1,0:T(8,128)S(1)}, u32[]{:S(2)}) copy-start(s32[1,1,512,4]{3,2,1,0:T(8,128)S(1)} %copy.30) | copy-start | bytes 24580
  338.3 7.7 %copy-start.1 = (bf16[2560,384]{1,0:T(8,128)(2,1)S(1)}, bf16[2560,384]{1,0:T(8,128)(2,1)}, u32[]{:S(2)}) copy-start(bf16[2560,384]{1,0:T(8,128)(2,1)} %get-tuple-element.54) | copy-start | bytes 5898244
  347.7 18.8 %copy-start.4 = (bf16[512,384]{1,0:T(8,128)(2,1)S(1)}, bf16[512,384]{1,0:T(8,128)(2,1)}, u32[]{:S(2)}) copy-start(bf16[512,384]{1,0:T(8,128)(2,1)} %get-tuple-element.51) | copy-start | bytes 1179652
  347.7 19.5 %copy-start.2 = (f32[512,384]{1,0:T(8,128)S(1)}, f32[512,384]{1,0:T(8,128)}, u32[]{:S(2)}) copy-start(f32[512,384]{1,0:T(8,128)} %get-tuple-element.52) | copy-start | bytes 2359300
